TPU v7x, 32 devices: a whole 2x2x4 slice. The times are simulated.
32 devices in a mesh: dp: 8 (over z, y), win: 4 (over x, core).
Axes of the slice: x: 2, y: 2, z: 4, core: 2. Of those that a mesh axis runs over, the one named last changes fastest.
Arguments:
- patches: bfloat16 [96, 4, 49, 768], P('dp', 'win'), may hold values from -6 to 6
- cotangent: bfloat16 [96, 4, 49, 768], P('dp', 'win'), may hold values from -6 to 6
- grid_sizes: int32 [96], P('dp'), may hold values from 7 to 12, as said below
- conv_weight: bfloat16 [3, 9, 768], P(None, None, 'dp'), may hold values from -2 to 2
- conv_bias: bfloat16 [3, 768], P(None, 'dp'), may hold values from -1.796875 to 1.796875
- norm_gain: bfloat16 [4, 768], P(None, 'dp'), may hold values from 0.25 to 1.75
- norm_bias: bfloat16 [4, 768], P(None, 'dp'), may hold values from -1.796875 to 1.796875
- qkv_weight: bfloat16 [2, 768, 2304], P(None, 'dp'), may hold values from -0.21875 to 0.21875
- spatial_bias: bfloat16 [1536], P('dp'), may hold values from -1.796875 to 1.796875
- channel_bias: bfloat16 [2304], P('dp'), may hold values from -1.796875 to 1.796875
- proj_weight: bfloat16 [2, 768, 768], P(None, 'dp'), may hold values from -0.625 to 0.625
- proj_bias: bfloat16 [2, 768], P(None, 'dp'), may hold values from -1.796875 to 1.796875
- hidden_weight: bfloat16 [2, 768, 3072], P(None, 'dp'), may hold values from -0.21875 to 0.21875
- hidden_bias: bfloat16 [2, 3072], P(None, 'dp'), may hold values from -1.796875 to 1.796875
- output_weight: bfloat16 [2, 3072, 768], P(None, 'dp'), may hold values from -0.109375 to 0.109375
- output_bias: bfloat16 [2, 768], P(None, 'dp'), may hold values from -1.796875 to 1.796875
Outputs:
- activations: bfloat16 [96, 4, 49, 768], P('dp', 'win')
- patches_grad: bfloat16 [96, 4, 49, 768], P('dp', 'win')
- conv_weight_grad: float32 [3, 9, 768], P(None, None, 'dp')
- conv_bias_grad: float32 [3, 768], P(None, 'dp')
- norm_gain_grad: float32 [4, 768], P(None, 'dp')
- norm_bias_grad: float32 [4, 768], P(None, 'dp')
- qkv_weight_grad: float32 [2, 768, 2304], P(None, 'dp')
- spatial_bias_grad: float32 [1536], P('dp')
- channel_bias_grad: float32 [2304], P('dp')
- proj_weight_grad: float32 [2, 768, 768], P(None, 'dp')
- proj_bias_grad: float32 [2, 768], P(None, 'dp')
- hidden_weight_grad: float32 [2, 768, 3072], P(None, 'dp')
- hidden_bias_grad: float32 [2, 3072], P(None, 'dp')
- output_weight_grad: float32 [2, 3072, 768], P(None, 'dp')
- output_bias_grad: float32 [2, 768], P(None, 'dp')
Inputs may be any that keep to these rules, and one draw needn't show every extreme that they name: `grid_sizes`: each image's grid side is 7, 9 or 12; among the 12 images of each index of dp at least one has side 12.
All inputs are finite; a program needn't handle non-finite values.
Results may differ from a plain program's by a relative error of at most 0.035.
Values may be sent and summed in bfloat16 or wider, within the bound.
A program may use at most 384 MiB of HBM per device.

v0:
```python
import jax
import jax.numpy as jnp
from jax import lax
from jax.sharding import PartitionSpec as P

HEADS = 24
HEAD = 32


EPS = 1e-05


def as_sent(array):
    return jax.tree.map(lambda a: a.astype(jnp.bfloat16) if a.dtype == jnp.float32 else a, array)


def image_valid(grid_sizes):
    rows = jnp.arange(7, dtype=jnp.int32)
    windows = jnp.arange(4, dtype=jnp.int32)
    top_rows = (windows // 2)[:, None] * 7 + rows[None, :]
    left_cols = (windows % 2)[:, None] * 7 + rows[None, :]
    sizes = grid_sizes[:, None, None, None]
    inside = (top_rows[None, :, :, None] < sizes) & (left_cols[None, :, None, :] < sizes)
    return inside.astype(jnp.float32).reshape(grid_sizes.shape[0], 4, 49, 1)


def layer_norm(stream, gain_row, shift_row):
    centre = jnp.mean(stream, -1, keepdims=True)
    centered = stream - centre
    variance = jnp.mean(centered * centered, -1, keepdims=True)
    return centered * lax.rsqrt(variance + EPS) * gain_row + shift_row


def gelu_exact(value_in):
    return jax.nn.gelu(value_in, approximate=False)


def matmul(left_rows, right_mat):
    return jnp.dot(left_rows, right_mat, preferred_element_type=jnp.float32)


def contract_rows(left_rows, right_rows):
    return lax.dot_general(
        left_rows, right_rows, (((0,), (0,)), ((), ())), preferred_element_type=jnp.float32
    )


def times_transposed(grad_rows, weight):
    return lax.dot_general(
        grad_rows, weight, (((1,), (1,)), ((), ())), preferred_element_type=jnp.float32
    )


def edge_lines(stream, images):
    channels = stream.shape[-1]
    image_grid = stream.reshape(images, 7, 7, channels)
    return jnp.stack(
        [image_grid[:, 0], image_grid[:, 6], image_grid[:, :, 0], image_grid[:, :, 6]], 1
    )[None]


def padded_tile(image_grid, lines, row_half, col_half):
    zero_line = jnp.zeros_like(lines[0, :, 0])
    upper = jnp.where(
        row_half == 1, jnp.where(col_half == 0, lines[0, :, 1], lines[1, :, 1]), zero_line
    )
    lower = jnp.where(
        row_half == 0, jnp.where(col_half == 0, lines[2, :, 0], lines[3, :, 0]), zero_line
    )
    left_side = jnp.where(
        col_half == 1, jnp.where(row_half == 0, lines[0, :, 3], lines[2, :, 3]), zero_line
    )
    right_side = jnp.where(
        col_half == 0, jnp.where(row_half == 0, lines[1, :, 2], lines[3, :, 2]), zero_line
    )
    zero_cell = zero_line[:, 0]
    top_left = jnp.where((row_half == 1) & (col_half == 1), lines[0, :, 1, 6], zero_cell)
    top_right = jnp.where((row_half == 1) & (col_half == 0), lines[1, :, 1, 0], zero_cell)
    bottom_left = jnp.where((row_half == 0) & (col_half == 1), lines[2, :, 0, 6], zero_cell)
    bottom_right = jnp.where((row_half == 0) & (col_half == 0), lines[3, :, 0, 0], zero_cell)
    middle = jnp.concatenate([left_side[:, :, None], image_grid, right_side[:, :, None]], 2)
    top_row = jnp.concatenate([top_left[:, None], upper, top_right[:, None]], 1)
    bottom_row = jnp.concatenate([bottom_left[:, None], lower, bottom_right[:, None]], 1)
    return jnp.concatenate([top_row[:, None], middle, bottom_row[:, None]], 1)


def position_conv(stream, images, window, weight9, shift_row, valid_rows):
    channels = stream.shape[-1]
    lines = lax.all_gather(as_sent(edge_lines(stream, images)), "win", axis=0, tiled=True)
    padded = padded_tile(stream.reshape(images, 7, 7, channels), lines, window // 2, window % 2)
    summed = jnp.zeros((images, 7, 7, channels), jnp.float32)
    for tap_index in range(9):
        row_shift, col_shift = divmod(tap_index, 3)
        summed = (
            summed
            + weight9[tap_index] * padded[:, row_shift : row_shift + 7, col_shift : col_shift + 7]
        )
    return (stream + valid_rows * (summed + shift_row).reshape(images * 49, channels), padded)


def position_conv_back(grad_stream, padded, images, window, weight9, valid_rows):
    channels = grad_stream.shape[-1]
    masked = valid_rows * grad_stream
    lines = lax.all_gather(as_sent(edge_lines(masked, images)), "win", axis=0, tiled=True)
    image_grid = masked.reshape(images, 7, 7, channels)
    grad_pad = padded_tile(image_grid, lines, window // 2, window % 2)
    summed = jnp.zeros((images, 7, 7, channels), jnp.float32)
    tap_grads = []
    for tap_index in range(9):
        row_shift, col_shift = divmod(tap_index, 3)
        summed = (
            summed
            + weight9[tap_index]
            * grad_pad[:, 2 - row_shift : 9 - row_shift, 2 - col_shift : 9 - col_shift]
        )
        tap_grads.append(
            jnp.sum(
                image_grid * padded[:, row_shift : row_shift + 7, col_shift : col_shift + 7],
                axis=(0, 1, 2),
            )
        )
    return (
        grad_stream + summed.reshape(grad_stream.shape),
        jnp.stack(tap_grads),
        jnp.sum(image_grid, axis=(0, 1, 2)),
    )


def mlp_forward(normed, weight_in, bias_in, weight_out, bias_out):
    activated = gelu_exact(matmul(normed, weight_in) + bias_in).astype(jnp.bfloat16)
    return matmul(activated, weight_out) + bias_out


def mlp_backward(normed, grad_stream, valid_rows, weight_in, bias_in, weight_out):
    hidden_pre = matmul(normed, weight_in) + bias_in
    activated, gelu_pull = jax.vjp(gelu_exact, hidden_pre)
    grad_branch = (valid_rows * grad_stream).astype(jnp.bfloat16)
    grad_weight_out = contract_rows(activated.astype(jnp.bfloat16), grad_branch)
    grad_bias_out = jnp.sum(grad_branch.astype(jnp.float32), 0)
    grad_pre = gelu_pull(times_transposed(grad_branch, weight_out))[0].astype(jnp.bfloat16)
    grad_weight_in = contract_rows(normed, grad_pre)
    grad_bias_in = jnp.sum(grad_pre.astype(jnp.float32), 0)
    return (
        times_transposed(grad_pre, weight_in),
        grad_weight_in,
        grad_bias_in,
        grad_weight_out,
        grad_bias_out,
    )


def norm_backward(stream, gain_row, shift_row, grad_normed):
    unused, norm_pull = jax.vjp(layer_norm, stream, gain_row, shift_row)
    return norm_pull(grad_normed)


def window_probs(packed, images, scaling, valid_rows):
    split = packed.reshape(images, 49, 3, HEADS, HEAD)
    query_rows = split[:, :, 0]
    key_rows = split[:, :, 1]
    value_rows = split[:, :, 2]
    key_ok = valid_rows.reshape(images, 1, 1, 49) > 0.5
    scores = (
        jnp.einsum("iphe,iqhe->ihpq", query_rows, key_rows, preferred_element_type=jnp.float32)
        * scaling
    )
    scores = jnp.where(key_ok, scores, -1000000000.0)
    return (query_rows, key_rows, value_rows, jax.nn.softmax(scores, axis=-1))


def channel_mixing(gram_total, scaling):
    return jax.nn.softmax(gram_total * scaling, axis=-1)


def channel_grads(
    grad_mixing, mixing, grad_context, key_masked, value_masked, valid_cells, scaling
):
    grad_query = jnp.einsum(
        "bgcd,bpgc->bpgd",
        mixing.astype(jnp.bfloat16),
        grad_context,
        preferred_element_type=jnp.float32,
    )
    grad_gram = (mixing * (grad_mixing - jnp.sum(mixing * grad_mixing, -1, keepdims=True))).astype(
        jnp.bfloat16
    )
    grad_keys = (
        jnp.einsum("bgcd,bpgd->bpgc", grad_gram, value_masked, preferred_element_type=jnp.float32)
        * scaling
        * valid_cells
    )
    grad_values = (
        jnp.einsum("bgcd,bpgc->bpgd", grad_gram, key_masked, preferred_element_type=jnp.float32)
        * scaling
        * valid_cells
    )
    return jnp.stack([grad_query, grad_keys, grad_values], 2).astype(jnp.bfloat16)


def on_device(
    patches,
    cotangent,
    grid_sizes,
    conv_weight,
    conv_bias,
    norm_gain,
    norm_bias,
    qkv_weight,
    spatial_bias,
    channel_bias,
    proj_weight,
    proj_bias,
    hidden_weight,
    hidden_bias,
    output_weight,
    output_bias,
):
    (
        conv_w,
        conv_b,
        gains,
        shifts,
        qkv_w,
        sp_bias,
        ch_bias,
        proj_w,
        proj_b,
        hid_w,
        hid_b,
        out_w,
        out_b,
    ) = (
        lax.all_gather(conv_weight, "dp", axis=2, tiled=True),
        lax.all_gather(conv_bias, "dp", axis=1, tiled=True),
        lax.all_gather(norm_gain, "dp", axis=1, tiled=True),
        lax.all_gather(norm_bias, "dp", axis=1, tiled=True),
        lax.all_gather(qkv_weight, "dp", axis=1, tiled=True),
        lax.all_gather(spatial_bias, "dp", axis=0, tiled=True),
        lax.all_gather(channel_bias, "dp", axis=0, tiled=True),
        lax.all_gather(proj_weight, "dp", axis=1, tiled=True),
        lax.all_gather(proj_bias, "dp", axis=1, tiled=True),
        lax.all_gather(hidden_weight, "dp", axis=1, tiled=True),
        lax.all_gather(hidden_bias, "dp", axis=1, tiled=True),
        lax.all_gather(output_weight, "dp", axis=1, tiled=True),
        lax.all_gather(output_bias, "dp", axis=1, tiled=True),
    )
    conv_w = conv_w.astype(jnp.float32)
    conv_b = conv_b.astype(jnp.float32)
    gains = gains.astype(jnp.float32)
    shifts = shifts.astype(jnp.float32)
    sp_bias = sp_bias.astype(jnp.float32)
    ch_bias = ch_bias.astype(jnp.float32)
    proj_b = proj_b.astype(jnp.float32)
    hid_b = hid_b.astype(jnp.float32)
    out_b = out_b.astype(jnp.float32)
    images = patches.shape[0]
    model_width = patches.shape[-1]
    rows_all = images * 49
    group_count = lax.axis_size("win")
    local_heads = HEADS // group_count
    group_width = model_width // group_count
    scaling = HEAD ** (-0.5)
    window = lax.axis_index("win")
    full_valid = image_valid(grid_sizes)
    valid_rows = lax.dynamic_slice_in_dim(full_valid, window, 1, 1).reshape(rows_all, 1)
    stream0 = patches.astype(jnp.float32).reshape(rows_all, model_width) * valid_rows
    stream1, pad_first = position_conv(stream0, images, window, conv_w[0], conv_b[0], valid_rows)
    normed1 = layer_norm(stream1, gains[0], shifts[0]).astype(jnp.bfloat16)
    packed_bias = jnp.concatenate(
        [sp_bias[:model_width], jnp.zeros((model_width,), jnp.float32), sp_bias[model_width:]]
    )
    packed1 = (matmul(normed1, qkv_w[0]) + packed_bias).astype(jnp.bfloat16)
    query1, keys1, values1, probs1 = window_probs(packed1, images, scaling, valid_rows)
    context1 = (
        jnp.einsum(
            "ihpq,iqhe->iphe",
            probs1.astype(jnp.bfloat16),
            values1,
            preferred_element_type=jnp.float32,
        )
        .astype(jnp.bfloat16)
        .reshape(rows_all, model_width)
    )
    stream2 = stream1 + valid_rows * (matmul(context1, proj_w[0]) + proj_b[0])
    stream3, pad_second = position_conv(stream2, images, window, conv_w[1], conv_b[1], valid_rows)
    normed3 = layer_norm(stream3, gains[1], shifts[1]).astype(jnp.bfloat16)
    stream4 = stream3 + valid_rows * mlp_forward(normed3, hid_w[0], hid_b[0], out_w[0], out_b[0])
    stream5, pad_third = position_conv(stream4, images, window, conv_w[2], conv_b[2], valid_rows)
    normed5 = layer_norm(stream5, gains[2], shifts[2]).astype(jnp.bfloat16)
    packed5 = (matmul(normed5, qkv_w[1]) + ch_bias).astype(jnp.bfloat16)
    moved = lax.all_to_all(
        packed5.reshape(images, 1, 49, 3, group_count, group_width),
        "win",
        split_axis=4,
        concat_axis=1,
        tiled=True,
    )
    grouped = moved.reshape(images, 196, 3, local_heads, HEAD)
    valid_cells = full_valid.reshape(images, 196, 1, 1)
    query5 = grouped[:, :, 0]
    key_masked = grouped[:, :, 1] * valid_cells.astype(jnp.bfloat16)
    value_masked = grouped[:, :, 2] * valid_cells.astype(jnp.bfloat16)
    gram_total = jnp.einsum(
        "bpgc,bpgd->bgcd", key_masked, value_masked, preferred_element_type=jnp.float32
    )
    mixing = channel_mixing(gram_total, scaling)
    context_groups = jnp.einsum(
        "bgcd,bpgd->bpgc", mixing.astype(jnp.bfloat16), query5, preferred_element_type=jnp.float32
    ).astype(jnp.bfloat16)
    returned = lax.all_to_all(
        context_groups.reshape(images, 4, 49, 1, group_width),
        "win",
        split_axis=1,
        concat_axis=3,
        tiled=True,
    )
    context5 = returned.reshape(rows_all, model_width)
    stream6 = stream5 + valid_rows * (matmul(context5, proj_w[1]) + proj_b[1])
    normed6 = layer_norm(stream6, gains[3], shifts[3]).astype(jnp.bfloat16)
    stream7 = stream6 + valid_rows * mlp_forward(normed6, hid_w[1], hid_b[1], out_w[1], out_b[1])
    activations = stream7.astype(jnp.bfloat16).reshape(patches.shape)
    grad7 = cotangent.astype(jnp.float32).reshape(rows_all, model_width)
    grad_normed, hid_w_grad1, hid_b_grad1, out_w_grad1, out_b_grad1 = mlp_backward(
        normed6, grad7, valid_rows, hid_w[1], hid_b[1], out_w[1]
    )
    grad_part, gain_grad3, shift_grad3 = norm_backward(stream6, gains[3], shifts[3], grad_normed)
    grad6 = grad7 + grad_part
    branch_grad = (valid_rows * grad6).astype(jnp.bfloat16)
    proj_w_grad1 = contract_rows(context5, branch_grad)
    proj_b_grad1 = jnp.sum(branch_grad.astype(jnp.float32), 0)
    context_grad = times_transposed(branch_grad, proj_w[1]).astype(jnp.bfloat16)
    moved_grad = lax.all_to_all(
        context_grad.reshape(images, 1, 49, group_count, group_width),
        "win",
        split_axis=3,
        concat_axis=1,
        tiled=True,
    )
    group_grad = moved_grad.reshape(images, 196, local_heads, HEAD)
    mixing_grad = jnp.einsum(
        "bpgc,bpgd->bgcd", group_grad, query5, preferred_element_type=jnp.float32
    )
    stacked = channel_grads(
        mixing_grad, mixing, group_grad, key_masked, value_masked, valid_cells, scaling
    )
    sent_back = lax.all_to_all(
        stacked.reshape(images, 4, 49, 3, 1, group_width),
        "win",
        split_axis=1,
        concat_axis=4,
        tiled=True,
    )
    packed_grad5 = sent_back.reshape(rows_all, 3 * model_width)
    qkv_w_grad1 = contract_rows(normed5, packed_grad5)
    ch_bias_grad = jnp.sum(packed_grad5.astype(jnp.float32), 0)
    grad_part, gain_grad2, shift_grad2 = norm_backward(
        stream5, gains[2], shifts[2], times_transposed(packed_grad5, qkv_w[1])
    )
    grad5 = grad6 + grad_part
    grad4, conv_w_grad2, conv_b_grad2 = position_conv_back(
        grad5, pad_third, images, window, conv_w[2], valid_rows
    )
    grad_normed, hid_w_grad0, hid_b_grad0, out_w_grad0, out_b_grad0 = mlp_backward(
        normed3, grad4, valid_rows, hid_w[0], hid_b[0], out_w[0]
    )
    grad_part, gain_grad1, shift_grad1 = norm_backward(stream3, gains[1], shifts[1], grad_normed)
    grad3 = grad4 + grad_part
    grad2, conv_w_grad1, conv_b_grad1 = position_conv_back(
        grad3, pad_second, images, window, conv_w[1], valid_rows
    )
    branch_grad = (valid_rows * grad2).astype(jnp.bfloat16)
    proj_w_grad0 = contract_rows(context1, branch_grad)
    proj_b_grad0 = jnp.sum(branch_grad.astype(jnp.float32), 0)
    context_grad = (
        times_transposed(branch_grad, proj_w[0])
        .astype(jnp.bfloat16)
        .reshape(images, 49, HEADS, HEAD)
    )
    probs_low = probs1.astype(jnp.bfloat16)
    probs_grad = jnp.einsum(
        "iphe,iqhe->ihpq", context_grad, values1, preferred_element_type=jnp.float32
    )
    values_grad = jnp.einsum(
        "ihpq,iphe->iqhe", probs_low, context_grad, preferred_element_type=jnp.float32
    )
    scores_grad = (probs1 * (probs_grad - jnp.sum(probs1 * probs_grad, -1, keepdims=True))).astype(
        jnp.bfloat16
    )
    key_ok = valid_rows.reshape(images, 1, 1, 49) > 0.5
    scores_grad = jnp.where(key_ok, scores_grad, jnp.zeros_like(scores_grad))
    query_grad = (
        jnp.einsum("ihpq,iqhe->iphe", scores_grad, keys1, preferred_element_type=jnp.float32)
        * scaling
    )
    keys_grad = (
        jnp.einsum("ihpq,iphe->iqhe", scores_grad, query1, preferred_element_type=jnp.float32)
        * scaling
    )
    packed_grad1 = (
        jnp.stack([query_grad, keys_grad, values_grad], 2)
        .astype(jnp.bfloat16)
        .reshape(rows_all, 3 * model_width)
    )
    qkv_w_grad0 = contract_rows(normed1, packed_grad1)
    packed_sums = jnp.sum(packed_grad1.astype(jnp.float32), 0)
    sp_bias_grad = jnp.concatenate([packed_sums[:model_width], packed_sums[2 * model_width :]])
    grad_part, gain_grad0, shift_grad0 = norm_backward(
        stream1, gains[0], shifts[0], times_transposed(packed_grad1, qkv_w[0])
    )
    grad1 = grad2 + grad_part
    grad0, conv_w_grad0, conv_b_grad0 = position_conv_back(
        grad1, pad_first, images, window, conv_w[0], valid_rows
    )
    patches_grad = (grad0 * valid_rows).astype(jnp.bfloat16).reshape(patches.shape)
    local_sums = (
        lax.psum_scatter(
            jnp.stack([conv_w_grad0, conv_w_grad1, conv_w_grad2]),
            "dp",
            scatter_dimension=2,
            tiled=True,
        ),
        lax.psum_scatter(
            jnp.stack([conv_b_grad0, conv_b_grad1, conv_b_grad2]),
            "dp",
            scatter_dimension=1,
            tiled=True,
        ),
        lax.psum_scatter(
            jnp.stack([gain_grad0, gain_grad1, gain_grad2, gain_grad3]),
            "dp",
            scatter_dimension=1,
            tiled=True,
        ),
        lax.psum_scatter(
            jnp.stack([shift_grad0, shift_grad1, shift_grad2, shift_grad3]),
            "dp",
            scatter_dimension=1,
            tiled=True,
        ),
        lax.psum_scatter(
            jnp.stack([qkv_w_grad0, qkv_w_grad1]), "dp", scatter_dimension=1, tiled=True
        ),
        lax.psum_scatter(sp_bias_grad, "dp", scatter_dimension=0, tiled=True),
        lax.psum_scatter(ch_bias_grad, "dp", scatter_dimension=0, tiled=True),
        lax.psum_scatter(
            jnp.stack([proj_w_grad0, proj_w_grad1]), "dp", scatter_dimension=1, tiled=True
        ),
        lax.psum_scatter(
            jnp.stack([proj_b_grad0, proj_b_grad1]), "dp", scatter_dimension=1, tiled=True
        ),
        lax.psum_scatter(
            jnp.stack([hid_w_grad0, hid_w_grad1]), "dp", scatter_dimension=1, tiled=True
        ),
        lax.psum_scatter(
            jnp.stack([hid_b_grad0, hid_b_grad1]), "dp", scatter_dimension=1, tiled=True
        ),
        lax.psum_scatter(
            jnp.stack([out_w_grad0, out_w_grad1]), "dp", scatter_dimension=1, tiled=True
        ),
        lax.psum_scatter(
            jnp.stack([out_b_grad0, out_b_grad1]), "dp", scatter_dimension=1, tiled=True
        ),
    )
    summed = (
        lax.psum(local_sums[0].astype(jnp.bfloat16), "win").astype(jnp.float32),
        lax.psum(local_sums[1].astype(jnp.bfloat16), "win").astype(jnp.float32),
        lax.psum(local_sums[2].astype(jnp.bfloat16), "win").astype(jnp.float32),
        lax.psum(local_sums[3].astype(jnp.bfloat16), "win").astype(jnp.float32),
        lax.psum(local_sums[4].astype(jnp.bfloat16), "win").astype(jnp.float32),
        lax.psum(local_sums[5].astype(jnp.bfloat16), "win").astype(jnp.float32),
        lax.psum(local_sums[6].astype(jnp.bfloat16), "win").astype(jnp.float32),
        lax.psum(local_sums[7].astype(jnp.bfloat16), "win").astype(jnp.float32),
        lax.psum(local_sums[8].astype(jnp.bfloat16), "win").astype(jnp.float32),
        lax.psum(local_sums[9].astype(jnp.bfloat16), "win").astype(jnp.float32),
        lax.psum(local_sums[10].astype(jnp.bfloat16), "win").astype(jnp.float32),
        lax.psum(local_sums[11].astype(jnp.bfloat16), "win").astype(jnp.float32),
        lax.psum(local_sums[12].astype(jnp.bfloat16), "win").astype(jnp.float32),
    )
    return (activations, patches_grad) + tuple(summed)


def solution(mesh):
    return jax.shard_map(
        on_device,
        mesh=mesh,
        in_specs=(
            P("dp", "win", None, None),
            P("dp", "win", None, None),
            P("dp"),
            P(None, None, "dp"),
            P(None, "dp"),
            P(None, "dp"),
            P(None, "dp"),
            P(None, "dp", None),
            P("dp"),
            P("dp"),
            P(None, "dp", None),
            P(None, "dp"),
            P(None, "dp", None),
            P(None, "dp"),
            P(None, "dp", None),
            P(None, "dp"),
        ),
        out_specs=(
            P("dp", "win", None, None),
            P("dp", "win", None, None),
            P(None, None, "dp"),
            P(None, "dp"),
            P(None, "dp"),
            P(None, "dp"),
            P(None, "dp", None),
            P("dp"),
            P("dp"),
            P(None, "dp", None),
            P(None, "dp"),
            P(None, "dp", None),
            P(None, "dp"),
            P(None, "dp", None),
            P(None, "dp"),
        ),
        check_vma=False,
    )
```

profile of v0, /device:TPU:0, one launch (start us, length us, event | category | flops | bytes accessed | tf_op | source)
XLA Modules:
  0.0 2636.1 jit_solution(9362558373858045179)
XLA Ops:
  19.3 33.8 %all_gather.57 = bf16[3,9,768]{1,0,2:T(4,128)(2,1)S(1)} all-gather(bf16[3,9,96]{1,0,2:T(4,128)(2,1)S(1)} %copy.3681), channel_id=1, replica_groups=mesh['dp'=8,'win'=4] {'dp'}, dimensions={2}, use_global_device_ids=true | all-gather | bytes 46656 | tf_op jit(solution)/shard_map/all_gather | solution.py:233
  53.3 19.7 slice_reduce_fusion.26
  73.1 56.9 %slice_reduce_fusion.8 = (f32[768]{0:T(1024)}, f32[768]{0:T(1024)}, f32[768]{0:T(1024)}, f32[768]{0:T(1024)}, f32[768]{0:T(1024)}, /*index=5*/f32[768]{0:T(1024)...) fusion(f32[3,9,768]{1,0,2:T(4,128)S(1)} %convert_element_type.647), kind=kLoop, calls=%fused_computation.351 | loop fusion | bytes 116736 | tf_op jit(solution)/shard_map/slice | solution.py:96
  134.8 20.7 all-gather.3
  156.6 33.4 %all-reduce.5 = (bf16[1536]{0:T(1024)(128)(2,1)S(1)}, bf16[2304]{0:T(1024)(128)(2,1)S(1)}) all-reduce(bf16[1536]{0:T(1024)(128)(2,1)S(1)} %dynamic-update-slice, bf16[2304]{0:T(1024)(128)(2,1)S(1)} %dynamic-update-slice.1), channel_id=1, replica_groups=mesh['dp'=8,'win'=4] {'dp'}, use_global_device_ids=true, to_apply=%add | all-reduce | flops 3840 | bytes 15360
  190.0 16.3 all-gather
  206.5 18.4 all-gather.1
  225.0 16.3 all-gather.2
  275.0 11.2 reshape.2561
  286.2 7.8 fusion.209
  337.1 18.2 all-gather.4
  355.4 26.3 all_gather.68
  403.8 93.7 %all-gather.24.cloned.1.call-done = bf16[2,768,3072]{2,1,0:T(8,128)(2,1)} async-done(((bf16[2,96,3072]{2,1,0:T(8,128)(2,1)}), bf16[2,768,3072]{2,1,0:T(8,128)(2,1)}) %all-gather.24.cloned.1.call-update) | async-done | bytes 9437200 | tf_op jit(solution)/shard_map/all_gather | solution.py:242
  497.5 22.3 multiply_convert_fusion.2
  519.8 116.0 %all-gather.26.cloned.1.call-done = bf16[2,3072,768]{2,1,0:T(8,128)(2,1)} async-done(((bf16[2,384,768]{2,1,0:T(8,128)(2,1)}), bf16[2,3072,768]{2,1,0:T(8,128)(2,1)}) %all-gather.26.cloned.1.call-update) | async-done | bytes 9437200 | tf_op jit(solution)/shard_map/all_gather | solution.py:244
  647.8 20.7 all-gather.28.cloned.1.call-done
  710.0 46.8 %all-to-all-done = bf16[12,1,49,3,4,192]{5,2,3,1,0,4:T(8,128)(2,1)} async-done(((bf16[12,1,49,3,4,192]{5,2,3,1,0,4:T(8,128)(2,1)}), bf16[12,1,49,3,4,192]{5,2,3,1,0,4:T(8,128)(2,1)}, u32[]{:S(2)}, u32[]{:S(2)}) %all-to-all-start) | async-done | bytes 2709536 | tf_op jit(solution)/shard_map/all_to_all | solution.py:291
  756.7 10.5 copy.3759
  767.2 9.1 reshape.2483
  800.5 12.0 all-to-all-done.1
  820.7 22.5 multiply_convert_fusion.1
  843.3 8.8 convert_reduce_fusion.2
  872.5 17.6 all-to-all-done.2
  916.1 9.5 pad_maximum_fusion.3
  925.6 11.9 copy.3769
  937.5 51.4 %all_to_all.60 = bf16[12,4,49,3,1,192]{5,2,4,3,0,1:T(8,128)(2,1)S(1)} all-to-all(bf16[12,4,49,3,1,192]{5,2,4,3,0,1:T(8,128)(2,1)} %copy.3769), channel_id=1, replica_groups=mesh['dp'=8,'win'=4] {'win'}, dimensions={1} | all-to-all | bytes 5419008 | tf_op jit(solution)/shard_map/all_to_all | solution.py:346
  1017.2 22.5 all-gather.30.cloned.1.call-done
  1056.9 10.5 convert_reduce_fusion.3
  1078.8 9.8 multiply_reduce_fusion.1
  1089.8 9.2 multiply_reduce_fusion.9
  1129.3 8.0 convert_bitcast_fusion
  1141.8 15.8 fusion.42
  1157.7 15.2 fusion.43
  1180.3 15.2 copy.3821
  1195.5 13.1 convert_element_type.717
  1220.1 9.3 multiply_reduce_fusion.17
  1248.8 8.6 convolution_bitcast_fusion.4
  1262.5 11.0 pad_maximum_fusion.2
  1324.7 37.5 %all-reduce.4 = (bf16[1536]{0:T(1024)(128)(2,1)S(1)}, bf16[2304]{0:T(1024)(128)(2,1)S(1)}) all-reduce(f32[1536]{0:T(1024)S(1)} %pad_maximum_fusion.36, f32[2304]{0:T(1024)S(1)} %reduce_sum.752), channel_id=7, replica_groups=mesh['dp'=8,'win'=4] {'dp'}, use_global_device_ids=true, to_apply=%region_71.72.clone | all-reduce | flops 3840 | bytes 23040
  1364.1 61.0 %reduce-scatter.40.cloned.1.call-done = f32[96,4]{1,0:T(8,128)} async-done(((f32[768,4]{1,0:T(8,128)}), f32[96,4]{1,0:T(8,128)}) %reduce-scatter.40.cloned.1.call-update) | async-done | bytes 1552
  1426.0 63.0 %reduce-scatter.38.cloned.1.call-done = f32[96,4]{1,0:T(8,128)} async-done(((f32[768,4]{1,0:T(8,128)}), f32[96,4]{1,0:T(8,128)}) %reduce-scatter.38.cloned.1.call-update) | async-done | bytes 1552
  1489.8 63.6 %reduce-scatter.34.cloned.1.call-done = f32[96,27]{1,0:T(8,128)} async-done(((f32[768,27]{1,0:T(8,128)}), f32[96,27]{1,0:T(8,128)}) %reduce-scatter.34.cloned.1.call-update) | async-done | bytes 10384
  1554.4 10.3 all-reduce.6
  1582.4 93.9 %reduce-scatter.28.cloned.1.call-done = f32[2,96,768]{2,1,0:T(8,128)} async-done(((f32[2,768,768]{2,1,0:T(8,128)}), f32[2,96,768]{2,1,0:T(8,128)}) %reduce-scatter.28.cloned.1.call-update) | async-done | bytes 589840 | tf_op jit(solution)/shard_map/reduce_scatter | solution.py:445
  1678.1 231.3 %reduce-scatter.26.cloned.1.call-done = f32[2,96,2304]{2,1,0:T(8,128)} async-done(((f32[2,768,2304]{2,1,0:T(8,128)}), f32[2,96,2304]{2,1,0:T(8,128)}) %reduce-scatter.26.cloned.1.call-update) | async-done | bytes 1769488 | tf_op jit(solution)/shard_map/reduce_scatter | solution.py:440
  1911.9 314.1 %reduce-scatter.30.cloned.1.call-done = f32[2,96,3072]{2,1,0:T(8,128)} async-done(((f32[2,768,3072]{2,1,0:T(8,128)}), f32[2,96,3072]{2,1,0:T(8,128)}) %reduce-scatter.30.cloned.1.call-update) | async-done | bytes 2359312 | tf_op jit(solution)/shard_map/reduce_scatter | solution.py:451
  2228.9 314.0 %reduce-scatter.32.cloned.1.call-done = f32[2,384,768]{2,1,0:T(8,128)} async-done(((f32[2,3072,768]{2,1,0:T(8,128)}), f32[2,384,768]{2,1,0:T(8,128)}) %reduce-scatter.32.cloned.1.call-update) | async-done | bytes 2359312 | tf_op jit(solution)/shard_map/reduce_scatter | solution.py:457
  2557.9 63.5 %all-reduce.10.cloned.1.call-done = (bf16[2,96,2304]{2,1,0:T(8,128)(2,1)}, bf16[2,96,768]{2,1,0:T(8,128)(2,1)}, bf16[2,96,3072]{2,1,0:T(8,128)(2,1)}, bf16[2,384,768]{2,1,0:T(8,128)(2,1)}) async-done(((bf16[2,96,2304]{2,1,0:T(8,128)(2,1)}, bf16[2,96,768]{2,1,0:T(8,128)(2,1)}, bf16[2,96,3072]{2,1,0:T(8,128)(2,1)}, bf16[2,384,768]{2,1,0:T(8,128)(2,1)}), (bf16[2,96,2304]{2,1,0:T(8,128)(2,1)}, ...) | async-done | bytes 3538960 | tf_op jit(solution)/shard_map/psum | solution.py:469
  (805 shorter events, 483.0 us)
Async XLA Ops:
  7.2 234.9 %all-gather.16.cloned.1.call-start = ((), (), s32[]{:S(2)}) async-start(), calls=%async_computation.15 | async-start | bytes 2580480 | tf_op jit(solution)/shard_map/all_gather | solution.py:89
  15.5 234.4 %copy-start.10 = (f32[12,7,7,768]{3,2,1,0:T(8,128)}, f32[12,7,7,768]{3,2,1,0:T(8,128)S(1)}, u32[]{:S(2)}) copy-start(f32[12,7,7,768]{3,2,1,0:T(8,128)S(1)} %get-tuple-element.539) | copy-start | bytes 5419012
  17.4 253.0 %all-gather.18.cloned.1.call-start = ((), (), s32[]{:S(2)}) async-start(), calls=%async_computation.16 | async-start | bytes 7962624 | tf_op jit(solution)/shard_map/all_gather | solution.py:237
  18.2 309.4 %all-gather.20.cloned.1.call-start = ((), (), s32[]{:S(2)}) async-start(), calls=%async_computation.17 | async-start | bytes 2654208 | tf_op jit(solution)/shard_map/all_gather | solution.py:240
  18.9 364.1 %all-gather.22.cloned.1.call-start = ((), (), s32[]{:S(2)}) async-start(), calls=%async_computation.18 | async-start | bytes 2580480 | tf_op jit(solution)/shard_map/all_gather | solution.py:89
  19.0 294.3 %copy-start.156 = (pred[12,49]{1,0:T(8,128)(4,1)}, pred[12,49]{1,0:T(8,128)(4,1)S(1)}, u32[]{:S(2)}) copy-start(pred[12,49]{1,0:T(8,128)(4,1)S(1)} %broadcast_compare_fusion.2) | copy-start | bytes 1768
  73.0 176.9 %copy-start.104 = (f32[768]{0:T(1024)}, f32[768]{0:T(1024)S(1)}, u32[]{:S(2)}) copy-start(f32[768]{0:T(1024)S(1)} %get-tuple-element.466) | copy-start | bytes 9220
  73.0 176.9 %copy-start.106 = (f32[768]{0:T(1024)}, f32[768]{0:T(1024)S(1)}, u32[]{:S(2)}) copy-start(f32[768]{0:T(1024)S(1)} %get-tuple-element.467) | copy-start | bytes 9220
  73.0 176.9 %copy-start.108 = (f32[768]{0:T(1024)}, f32[768]{0:T(1024)S(1)}, u32[]{:S(2)}) copy-start(f32[768]{0:T(1024)S(1)} %get-tuple-element.468) | copy-start | bytes 9220
  73.0 176.9 %copy-start.110 = (f32[768]{0:T(1024)}, f32[768]{0:T(1024)S(1)}, u32[]{:S(2)}) copy-start(f32[768]{0:T(1024)S(1)} %get-tuple-element.469) | copy-start | bytes 9220
  73.1 176.9 %copy-start.112 = (f32[768]{0:T(1024)}, f32[768]{0:T(1024)S(1)}, u32[]{:S(2)}) copy-start(f32[768]{0:T(1024)S(1)} %get-tuple-element.470) | copy-start | bytes 9220
  73.1 176.9 %copy-start.114 = (f32[768]{0:T(1024)}, f32[768]{0:T(1024)S(1)}, u32[]{:S(2)}) copy-start(f32[768]{0:T(1024)S(1)} %get-tuple-element.471) | copy-start | bytes 9220
  73.1 176.9 %copy-start.116 = (f32[768]{0:T(1024)}, f32[768]{0:T(1024)S(1)}, u32[]{:S(2)}) copy-start(f32[768]{0:T(1024)S(1)} %get-tuple-element.472) | copy-start | bytes 9220
  129.9 261.2 %copy-start.122 = (f32[768]{0:T(1024)}, f32[768]{0:T(1024)S(1)}, u32[]{:S(2)}) copy-start(f32[768]{0:T(1024)S(1)} %get-tuple-element.456) | copy-start | bytes 9220
  130.0 261.3 %copy-start.124 = (f32[768]{0:T(1024)}, f32[768]{0:T(1024)S(1)}, u32[]{:S(2)}) copy-start(f32[768]{0:T(1024)S(1)} %get-tuple-element.457) | copy-start | bytes 9220
  130.0 261.3 %copy-start.126 = (f32[768]{0:T(1024)}, f32[768]{0:T(1024)S(1)}, u32[]{:S(2)}) copy-start(f32[768]{0:T(1024)S(1)} %get-tuple-element.458) | copy-start | bytes 9220
  130.0 261.3 %copy-start.128 = (f32[768]{0:T(1024)}, f32[768]{0:T(1024)S(1)}, u32[]{:S(2)}) copy-start(f32[768]{0:T(1024)S(1)} %get-tuple-element.459) | copy-start | bytes 9220
  130.0 261.3 %copy-start.130 = (f32[768]{0:T(1024)}, f32[768]{0:T(1024)S(1)}, u32[]{:S(2)}) copy-start(f32[768]{0:T(1024)S(1)} %get-tuple-element.460) | copy-start | bytes 9220
  130.0 261.3 %copy-start.132 = (f32[768]{0:T(1024)}, f32[768]{0:T(1024)S(1)}, u32[]{:S(2)}) copy-start(f32[768]{0:T(1024)S(1)} %get-tuple-element.461) | copy-start | bytes 9220
  130.0 261.3 %copy-start.134 = (f32[768]{0:T(1024)}, f32[768]{0:T(1024)S(1)}, u32[]{:S(2)}) copy-start(f32[768]{0:T(1024)S(1)} %get-tuple-element.462) | copy-start | bytes 9220
  130.0 261.3 %copy-start.136 = (f32[768]{0:T(1024)}, f32[768]{0:T(1024)S(1)}, u32[]{:S(2)}) copy-start(f32[768]{0:T(1024)S(1)} %get-tuple-element.463) | copy-start | bytes 9220
  130.0 261.3 %copy-start.138 = (f32[768]{0:T(1024)}, f32[768]{0:T(1024)S(1)}, u32[]{:S(2)}) copy-start(f32[768]{0:T(1024)S(1)} %get-tuple-element.464) | copy-start | bytes 9220
  242.0 255.5 %copy-start.79 = (f32[768]{0:T(1024)}, f32[768]{0:T(1024)S(1)}, u32[]{:S(2)}) copy-start(f32[768]{0:T(1024)S(1)} %get-tuple-element.664) | copy-start | bytes 9220
  242.0 255.5 %copy-start.87 = (f32[768]{0:T(1024)}, f32[768]{0:T(1024)S(1)}, u32[]{:S(2)}) copy-start(f32[768]{0:T(1024)S(1)} %get-tuple-element.480) | copy-start | bytes 9220
  335.9 161.6 %all-gather.24.cloned.1.call-start = ((), (), s32[]{:S(2)}) async-start(), calls=%async_computation.19 | async-start | bytes 10616832 | tf_op jit(solution)/shard_map/all_gather | solution.py:242
  336.5 299.3 %all-gather.26.cloned.1.call-start = ((), (), s32[]{:S(2)}) async-start(), calls=%async_computation.20 | async-start | bytes 10616832 | tf_op jit(solution)/shard_map/all_gather | solution.py:244
  337.1 331.4 %all-gather.28.cloned.1.call-start = ((), (), s32[]{:S(2)}) async-start(), calls=%async_computation.21 | async-start | bytes 2580480 | tf_op jit(solution)/shard_map/all_gather | solution.py:89
  403.5 232.4 %copy-start.11 = (f32[588,768]{1,0:T(8,128)}, f32[588,768]{1,0:T(8,128)S(1)}, u32[]{:S(2)}) copy-start(f32[588,768]{1,0:T(8,128)S(1)} %get-tuple-element.537) | copy-start | bytes 5419012
  688.8 319.8 %copy-start.98 = (f32[588]{0:T(1024)}, f32[588]{0:T(1024)S(1)}, u32[]{:S(2)}) copy-start(f32[588]{0:T(1024)S(1)} %broadcast_multiply_fusion.6) | copy-start | bytes 7060
  704.2 52.5 %all-to-all-start = ((bf16[12,1,49,3,4,192]{5,2,3,1,0,4:T(8,128)(2,1)}), bf16[12,1,49,3,4,192]{5,2,3,1,0,4:T(8,128)(2,1)}, u32[]{:S(2)}, u32[]{:S(2)}) async-start(bf16[12,1,49,3,4,192]{5,2,3,1,0,4:T(8,128)(2,1)} %copy.3758), calls=%async_computation | async-start | bytes 8257536 | tf_op jit(solution)/shard_map/all_to_all | solution.py:291
  790.5 22.0 all-to-all-start.1
  797.8 211.6 %copy-start.23 = (f32[588,768]{1,0:T(8,128)}, f32[588,768]{1,0:T(8,128)S(1)}, u32[]{:S(2)}) copy-start(f32[588,768]{1,0:T(8,128)S(1)} %reshape.2487) | copy-start | bytes 5419012
  868.6 21.5 all-to-all-start.2
  872.2 167.6 %all-gather.30.cloned.1.call-start = ((), (), s32[]{:S(2)}) async-start(), calls=%async_computation.22 | async-start | bytes 2580480 | tf_op jit(solution)/shard_map/all_gather | solution.py:104
  1017.2 83.8 %all-gather.32.cloned.1.call-start = ((), (), s32[]{:S(2)}) async-start(), calls=%async_computation.23 | async-start | bytes 2580480 | tf_op jit(solution)/shard_map/all_gather | solution.py:104
  1078.4 244.2 %reduce-scatter.46.cloned.1.call-start = ((), (), s32[]{:S(2)}) async-start(), calls=%async_computation.35 | async-start | bytes 442368
  1099.0 224.5 %reduce-scatter.44.cloned.1.call-start = ((), (), s32[]{:S(2)}) async-start(), calls=%async_computation.34 | async-start | bytes 1769472
  1100.9 261.5 %reduce-scatter.42.cloned.1.call-start = ((), (), s32[]{:S(2)}) async-start(), calls=%async_computation.33 | async-start | bytes 442368
  1231.7 131.5 %reduce-scatter.36.cloned.1.call-start = ((), (), s32[]{:S(2)}) async-start(), calls=%async_computation.30 | async-start | bytes 442368
  1232.7 192.4 %reduce-scatter.40.cloned.1.call-start = ((), (), s32[]{:S(2)}) async-start(), calls=%async_computation.32 | async-start | bytes 442368
  1233.8 255.1 %reduce-scatter.38.cloned.1.call-start = ((), (), s32[]{:S(2)}) async-start(), calls=%async_computation.31 | async-start | bytes 442368
  1234.9 318.4 %reduce-scatter.34.cloned.1.call-start = ((), (), s32[]{:S(2)}) async-start(), calls=%async_computation.29 | async-start | bytes 442368
  1239.1 337.9 %all-gather.34.cloned.1.call-start = ((), (), s32[]{:S(2)}) async-start(), calls=%async_computation.24 | async-start | bytes 2580480 | tf_op jit(solution)/shard_map/all_gather | solution.py:104
  1241.7 434.7 %reduce-scatter.28.cloned.1.call-start = ((), (), s32[]{:S(2)}) async-start(), calls=%async_computation.26 | async-start | bytes 5308416 | tf_op jit(solution)/shard_map/reduce_scatter | solution.py:445
  1248.1 661.3 %reduce-scatter.26.cloned.1.call-start = ((), (), s32[]{:S(2)}) async-start(), calls=%async_computation.25 | async-start | bytes 15925248 | tf_op jit(solution)/shard_map/reduce_scatter | solution.py:440
  1273.6 952.5 %reduce-scatter.30.cloned.1.call-start = ((), (), s32[]{:S(2)}) async-start(), calls=%async_computation.27 | async-start | bytes 21233664 | tf_op jit(solution)/shard_map/reduce_scatter | solution.py:451
  1292.3 1250.6 %reduce-scatter.32.cloned.1.call-start = ((), (), s32[]{:S(2)}) async-start(), calls=%async_computation.28 | async-start | bytes 21233664 | tf_op jit(solution)/shard_map/reduce_scatter | solution.py:457
  1310.1 1311.3 %all-reduce.10.cloned.1.call-start = ((), (), s32[]{:S(2)}) async-start(), calls=%async_computation.36 | async-start | bytes 7077888 | tf_op jit(solution)/shard_map/psum | solution.py:469
  (156 other events, 2024.6 us)
Sparse Core Ops, SparseCore 0:
  17.5 25.0 all-gather.15
  44.8 108.8 all-gather.17
  155.9 50.6 all-gather.19
  336.0 21.2 all-gather.21
  359.3 138.1 all-gather.23
  499.6 136.2 all-gather.25
  647.9 20.5 all-gather.27
  1017.3 22.3 all-gather.29
  1078.5 22.3 all-gather.31
  1104.1 61.3 reduce-scatter.45
  1168.9 63.8 reduce-scatter.43
  1236.3 60.3 reduce-scatter.41
  1300.8 60.3 reduce-scatter.35
  1364.7 60.3 reduce-scatter.39
  1428.6 60.3 reduce-scatter.37
  1493.0 60.3 reduce-scatter.33
  1555.4 21.5 all-gather.33
  1580.9 95.3 reduce-scatter.27
  1680.4 228.9 reduce-scatter.25
  1913.6 312.3 reduce-scatter.29
  2230.4 312.4 reduce-scatter.31
  2546.8 74.5 all-reduce.9
where the time goes:
time: 2650 us; the launch traced here: 2640 us
  waiting for transfers between devices  1540 us (58%)
  local copies, waits for them, and re-layouts  352 us (13%)
  blocking collectives  283 us (11%)
  matrix products  222 us (8%)
  other arithmetic  201 us (8%)
    reduce_scatter x1, waiting for transfers between devices, on_device(): lax.psum_scatter(jnp.stack([hid_w_grad0, hid_w_grad1]), 'dp', scatter_dim...  314 us
    reduce_scatter x1, waiting for transfers between devices, on_device(): lax.psum_scatter(jnp.stack([out_w_grad0, out_w_grad1]), 'dp', scatter_dim...  314 us
    reduce_scatter x1, waiting for transfers between devices, on_device(): lax.psum_scatter(jnp.stack([qkv_w_grad0, qkv_w_grad1]), 'dp', scatter_dim...  231 us
    unnamed x29, waiting for transfers between devices  190 us
    all_gather x1, waiting for transfers between devices, on_device(): lax.all_gather(output_weight, 'dp', axis=1, tiled=True)  116 us
    reduce_scatter x1, waiting for transfers between devices, on_device(): lax.psum_scatter(jnp.stack([proj_w_grad0, proj_w_grad1]), 'dp', scatter_d...  93.9 us
    all_gather x1, waiting for transfers between devices, on_device(): lax.all_gather(hidden_weight, 'dp', axis=1, tiled=True)  93.7 us
    slice x2, local copies, waits for them, and re-layouts, position_conv(): weight9[tap_index]  76.6 us
  transfers between devices with their start and end apart: 25, of which 16 were waited for; matrix products, arithmetic and copies ran while one was open for 18% of the time, Pallas kernels for 0%

commit v1 on v0

--- a/solution.py
+++ b/solution.py
@@ -1,13 +1,666 @@
+import functools
+
 import jax
 import jax.numpy as jnp
 from jax import lax
+from jax.experimental import pallas as pl
+from jax.experimental.pallas import tpu as pltpu
 from jax.sharding import PartitionSpec as P
 
 HEADS = 24
 HEAD = 32
-
-
 EPS = 1e-05
+MESH = pl.DeviceIdType.MESH
+F32 = jnp.float32
+BF16 = jnp.bfloat16
+SCALE = HEAD ** (-0.5)
+CELLS = 56
+PAIR = 112
+
+
+def dot(left, right):
+    return jnp.dot(left, right, preferred_element_type=F32)
+
+
+def dot_t(left, right):
+    return lax.dot_general(left, right, (((1,), (1,)), ((), ())), preferred_element_type=F32)
+
+
+def t_dot(left, right):
+    return lax.dot_general(left, right, (((0,), (0,)), ((), ())), preferred_element_type=F32)
+
+
+def iota(shape, dim):
+    return lax.broadcasted_iota(jnp.int32, shape, dim)
+
+
+def rows_at(index, count):
+    return pl.ds(pl.multiple_of(index * count, count), count)
+
+
+def lanes_at(index, count, base=0):
+    return pl.ds(pl.multiple_of(base + index * count, 128), count)
+
+
+def each(count, body):
+    def step(i, carry):
+        body(i)
+        return carry
+
+    lax.fori_loop(0, count, step, 0)
+
+
+def gelu_pair(pre):
+    t = 1.0 / (1.0 + 0.23164190 * jnp.abs(pre))
+    e = jnp.exp(-0.5 * pre * pre)
+    poly = (((1.061405429 * t - 1.453152027) * t + 1.421413741) * t - 0.284496736) * t + 0.254829592
+    tail = 0.5 * poly * t * e
+    cdf = jnp.where(pre >= 0.0, 1.0 - tail, tail)
+    return pre * cdf, cdf + pre * (e * 0.3989422804014327)
+
+
+def place():
+    d = lax.axis_index("dp")
+    w = lax.axis_index("win")
+    return d, w, w // 2, w % 2
+
+
+def greet(peers):
+    barrier = pltpu.get_barrier_semaphore()
+    for peer in peers:
+        pl.semaphore_signal(barrier, inc=1, device_id=peer, device_id_type=MESH)
+    pl.semaphore_wait(barrier, len(peers))
+
+
+def remote(src, dst, sems, peer):
+    return pltpu.make_async_remote_copy(
+        src_ref=src, dst_ref=dst, send_sem=sems.at[0], recv_sem=sems.at[1], device_id=peer, device_id_type=MESH
+    )
+
+
+def fill_valid(valid, sizes, images, wr, wc):
+    def one(i):
+        cell = iota((CELLS, 128), 0)
+        r, c = cell >> 3, cell & 7
+        inside = (r + 7 * wr < sizes[i]) & (c + 7 * wc < sizes[i]) & (c < 7)
+        valid[rows_at(i, CELLS), :] = jnp.where(inside, 1.0, 0.0).astype(F32)
+
+    each(images, one)
+
+
+def spread(valid_rows, width):
+    return jnp.concatenate([valid_rows] * (width // 128), axis=1)
+
+
+def halo(pad, images, wr, wc, row_out, row_in, col_out, col_in, sems, vertical, horizontal):
+    edge = 7 - 6 * wr
+
+    def pack(p):
+        one = pad[pl.ds(pl.multiple_of((18 * p + edge) * 8, 8), 8), :]
+        two = pad[pl.ds(pl.multiple_of((18 * p + 9 + edge) * 8, 8), 8), :]
+        row_out[rows_at(p, 16), :] = jnp.concatenate([one, two], axis=0).astype(BF16)
+
+    each(images // 2, pack)
+    copy = remote(row_out, row_in, sems.at[0], vertical)
+    copy.start()
+    copy.wait()
+    border = 8 - 8 * wr
+
+    def unpack(p):
+        both = row_in[rows_at(p, 16), :].astype(F32)
+        pad[pl.ds(pl.multiple_of((18 * p + border) * 8, 8), 8), :] = both[:8]
+        pad[pl.ds(pl.multiple_of((18 * p + 9 + border) * 8, 8), 8), :] = both[8:]
+
+    each(images // 2, unpack)
+    turn = 2 - 2 * wc
+    sub = iota((8, 128), 0)
+
+    def row_of(i, s):
+        at_row = border if s == 7 else s + 1
+        return pl.ds(pl.multiple_of((9 * i + at_row) * 8, 8), 8)
+
+    def pack_col(p):
+        for part in range(pad.shape[1] // 128):
+            at = pl.ds(part * 128, 128)
+            both = []
+            for i in (2 * p, 2 * p + 1):
+                line = jnp.zeros((8, 128), F32)
+                for s in range(8):
+                    line = jnp.where(sub == s, pltpu.roll(pad[row_of(i, s), at], s + turn, 0), line)
+                both.append(line)
+            col_out[rows_at(p, 16), at] = jnp.concatenate(both, axis=0).astype(BF16)
+
+    each(images // 2, pack_col)
+    copy = remote(col_out, col_in, sems.at[1], horizontal)
+    copy.start()
+    copy.wait()
+
+    def unpack_col(p):
+        for part in range(pad.shape[1] // 128):
+            at = pl.ds(part * 128, 128)
+            both = col_in[rows_at(p, 16), at].astype(F32)
+            for one in range(2):
+                line = both[8 * one : 8 * one + 8]
+                for s in range(8):
+                    to = row_of(2 * p + one, s)
+                    pad[to, at] = jnp.where(sub == 7, pltpu.roll(line, 7 - s, 0), pad[to, at])
+
+    each(images // 2, unpack_col)
+
+
+def side_masks(wr, wc):
+    c = iota((8, 128), 0)
+    left = jnp.where((c == 0) & (wc == 0), 0.0, 1.0).astype(F32)
+    right = jnp.where((c == 6) & (wc == 1), 0.0, 1.0).astype(F32)
+    return left, right
+
+
+def three(pad, i, at, left, right):
+    rows = [pad[pl.ds(pl.multiple_of((9 * i + r) * 8, 8), 8), at] for r in range(9)]
+    return [(pltpu.roll(v, 1, 0) * left, v, pltpu.roll(v, 7, 0) * right) for v in rows]
+
+
+def conv_forward(pad, images, vec, k, valid, out, left, right):
+    def one(i):
+        for part in range(pad.shape[1] // 128):
+            at = pl.ds(part * 128, 128)
+            moved = three(pad, i, at, left, right)
+            bias = vec[27 + k : 28 + k, at]
+            taps = [vec[9 * k + t : 9 * k + t + 1, at] for t in range(9)]
+            for r in range(7):
+                total = jnp.broadcast_to(bias, (8, 128))
+                for t in range(9):
+                    total = total + taps[t] * moved[r + t // 3][t % 3]
+                to = pl.ds(pl.multiple_of((7 * i + r) * 8, 8), 8)
+                out[to, at] = moved[r + 1][1] + valid[to, :] * total
+
+    each(images, one)
+
+
+def norm_rows(src, images, vec, k, dst):
+    gain = vec[30 + k : 31 + k, :]
+    shift = vec[34 + k : 35 + k, :]
+
+    def one(p):
+        x = src[rows_at(p, PAIR), :]
+        centered = x - jnp.mean(x, -1, keepdims=True)
+        variance = jnp.mean(centered * centered, -1, keepdims=True)
+        dst[rows_at(p, PAIR), :] = (centered * lax.rsqrt(variance + EPS) * gain + shift).astype(BF16)
+
+    each(images // 2, one)
+
+
+def to_pad(pad, p, rows):
+    pad[pl.ds(pl.multiple_of((18 * p + 1) * 8, 8), CELLS), :] = rows[:CELLS]
+    pad[pl.ds(pl.multiple_of((18 * p + 10) * 8, 8), CELLS), :] = rows[CELLS:]
+
+
+def of_pad(pad, p):
+    return jnp.concatenate(
+        [
+            pad[pl.ds(pl.multiple_of((18 * p + 1) * 8, 8), CELLS), :],
+            pad[pl.ds(pl.multiple_of((18 * p + 10) * 8, 8), CELLS), :],
+        ],
+        axis=0,
+    )
+
+
+def clear_borders(pad, images):
+    zero = jnp.zeros((8, pad.shape[1]), F32)
+
+    def one(i):
+        pad[pl.ds(pl.multiple_of(72 * i, 8), 8), :] = zero
+        pad[pl.ds(pl.multiple_of(72 * i + 64, 8), 8), :] = zero
+
+    each(images, one)
+
+
+def head_masks(kind):
+    lane = iota((PAIR, 128), 1) >> 5
+    return [jnp.where(lane == h, 1.0, 0.0).astype(F32).astype(kind) for h in range(4)]
+
+
+def pair_mask(sizes, p, wr, wc):
+    row = iota((PAIR, PAIR), 0)
+    lane = iota((PAIR, PAIR), 1)
+    second = lane >= CELLS
+    cell = jnp.where(second, lane - CELLS, lane)
+    side = jnp.where(second, sizes[2 * p + 1], sizes[2 * p])
+    r, c = cell >> 3, cell & 7
+    inside = (r + 7 * wr < side) & (c + 7 * wc < side) & (c < 7)
+    return inside & (second == (row >= CELLS))
+
+
+def stacked(value, masks):
+    return jnp.concatenate([value * m for m in masks], axis=0)
+
+
+def folded(value, masks):
+    total = value[:PAIR] * masks[0]
+    for h in range(1, 4):
+        total = total + value[h * PAIR : (h + 1) * PAIR] * masks[h]
+    return total
+
+
+def pair_probs(query_bd, key, allowed):
+    scores = dot_t(query_bd, key) * SCALE
+    scores = jnp.where(allowed, scores, -1000000000.0)
+    e = jnp.exp(scores - jnp.max(scores, -1, keepdims=True))
+    return e * (1.0 / jnp.sum(e, -1, keepdims=True))
+
+
+def window_attention(packed, images, sizes, wr, wc, context):
+    width = context.shape[1]
+
+    def pair(p):
+        rows = rows_at(p, PAIR)
+        allowed = jnp.concatenate([pair_mask(sizes, p, wr, wc).astype(F32)] * 4, axis=0) > 0.5
+        low = head_masks(BF16)
+        full = head_masks(F32)
+
+        def group(g):
+            query = packed[rows, lanes_at(g, 128)]
+            key = packed[rows, lanes_at(g, 128, width)]
+            value = packed[rows, lanes_at(g, 128, 2 * width)]
+            probs = pair_probs(stacked(query, low), key, allowed).astype(BF16)
+            context[rows, lanes_at(g, 128)] = folded(dot(probs, value), full).astype(BF16)
+
+        each(width // 128, group)
+
+    each(images // 2, pair)
+
+
+def image_halves(kind):
+    row = iota((PAIR, 128), 0)
+    first = jnp.where(row < CELLS, 1.0, 0.0).astype(F32)
+    return first.astype(kind), (1.0 - first).astype(kind)
+
+
+def fold_heads(square):
+    lane = iota((32, 128), 1) >> 5
+    total = jnp.zeros((32, 128), F32)
+    for h in range(4):
+        total = total + jnp.where(lane == h, square[32 * h : 32 * h + 32], 0.0)
+    return total
+
+
+def unfold_heads(block):
+    lane = iota((32, 128), 1) >> 5
+    return jnp.concatenate([jnp.where(lane == h, block, 0.0) for h in range(4)], axis=0)
+
+
+def pair_grams(left, left_base, right, right_base, images, valid, out):
+    def pair(p):
+        rows = rows_at(p, PAIR)
+        one, two = image_halves(BF16)
+        ok = valid[rows, :].astype(BF16)
+        one, two = one * ok, two * ok
+
+        def group(g):
+            a = left[rows, lanes_at(g, 128, left_base)]
+            b = right[rows, lanes_at(g, 128, right_base)]
+            both = t_dot(a, jnp.concatenate([b * one, b * two], axis=1))
+            out[pl.ds(pl.multiple_of(64 * p, 32), 32), lanes_at(g, 128)] = fold_heads(both[:, :128])
+            out[pl.ds(pl.multiple_of(64 * p + 32, 32), 32), lanes_at(g, 128)] = fold_heads(both[:, 128:])
+
+        each(out.shape[1] // 128, group)
+
+    each(images // 2, pair)
+
+
+def sum_windows(gram, ins, images, c, sems, vertical, horizontal):
+    half = images * 16
+    mine = pl.ds(pl.multiple_of(half * c, 32), half)
+
+    def add(ref, rows):
+        gram[rows, :] = gram[rows, :] + ref[rows, :]
+
+    copy = remote(gram, ins.at[0], sems.at[0], horizontal)
+    copy.start()
+    copy.wait()
+    each(images, lambda i: add(ins.at[0], rows_at(i, 32)))
+    copy = remote(gram.at[mine], ins.at[1, mine], sems.at[1], vertical)
+    copy.start()
+    copy.wait()
+    each(images // 2, lambda i: add(ins.at[1], pl.ds(pl.multiple_of(half * c + 32 * i, 32), 32)))
+    copy = remote(gram.at[mine], ins.at[2, mine], sems.at[2], horizontal)
+    copy.start()
+    copy.wait()
+    other = half * (1 - c)
+
+    def take(i):
+        rows = pl.ds(pl.multiple_of(other + 32 * i, 32), 32)
+        gram[rows, :] = ins[2, rows, :]
+
+    each(images // 2, take)
+
+
+def forward_kernel(
+    images,
+    width,
+    hidden,
+    sizes,
+    patches,
+    vec,
+    qbias,
+    hbias,
+    qkv0,
+    qkv1,
+    proj0,
+    proj1,
+    hid0,
+    hid1,
+    outw0,
+    outw1,
+    activations,
+    o_pad,
+    o_stream,
+    o_normed,
+    o_packed,
+    o_context,
+    o_act,
+    o_slope,
+    o_mix,
+    pad,
+    streams,
+    normed,
+    packed,
+    context,
+    act,
+    slope,
+    gram,
+    gram_in,
+    valid,
+    pre,
+    wq,
+    wp,
+    wh,
+    wo,
+    row_out,
+    row_in,
+    col_out,
+    col_in,
+    final,
+    halo_sems,
+    gram_sems,
+    load_sems,
+    save_sems,
+):
+    d, w, wr, wc = place()
+    n_rows = images * CELLS
+    pairs = images // 2
+    horizontal = (d, 2 * wr + 1 - wc)
+    vertical = (d, 2 * (1 - wr) + wc)
+    greet([horizontal, vertical])
+    left, right = side_masks(wr, wc)
+
+    loads = {}
+    for name, src, dst, s in (("q0", qkv0, wq, 0), ("p0", proj0, wp, 1), ("h0", hid0, wh, 2), ("o0", outw0, wo, 3)):
+        loads[name] = pltpu.make_async_copy(src, dst, load_sems.at[s])
+        loads[name].start()
+
+    def reload(name, src, dst, s):
+        loads[name] = pltpu.make_async_copy(src, dst, load_sems.at[s])
+        loads[name].start()
+
+    saves = {}
+
+    def save(name, src, dst, s):
+        saves[name] = pltpu.make_async_copy(src, dst, save_sems.at[s])
+        saves[name].start()
+
+    fill_valid(valid, sizes, images, wr, wc)
+    clear_borders(pad, images)
+
+    def enter(p):
+        rows = rows_at(p, PAIR)
+        to_pad(pad, p, patches[rows, :].astype(F32) * spread(valid[rows, :], width))
+
+    each(pairs, enter)
+
+    def convolve(k, stream):
+        halo(pad, images, wr, wc, row_out.at[k], row_in.at[k], col_out.at[k], col_in.at[k], halo_sems.at[k], vertical, horizontal)
+        conv_forward(pad, images, vec, k, valid, stream, left, right)
+
+    def qkv(k, x):
+        def tile(j):
+            at = lanes_at(j, 256)
+            packed[:, at] = (dot(x[...], wq[:, at]) + qbias[k : k + 1, at]).astype(BF16)
+
+        each(3 * width // 256, tile)
+
+    def proj(k, stream, store):
+        def tile(j):
+            at = lanes_at(j, 256)
+            pre[...] = dot(context[...], wp[:, at])
+
+            def part(p):
+                rows = rows_at(p, PAIR)
+                store(p, at, stream[rows, at] + spread(valid[rows, :], 256) * (pre[rows, :] + vec[38 + k : 39 + k, at]))
+
+            each(pairs, part)
+
+        each(width // 256, tile)
+
+    def feed_forward(k, x, stream, store):
+        def tile(j):
+            at = lanes_at(j, 256)
+            pre[...] = dot(x[...], wh[:, at])
+
+            def part(p):
+                rows = rows_at(p, PAIR)
+                a, s = gelu_pair(pre[rows, :] + hbias[k : k + 1, at])
+                act[rows, at] = a.astype(BF16)
+                slope[rows, at] = s.astype(BF16)
+
+            each(pairs, part)
+
+        each(hidden // 256, tile)
+
+        def tile2(j):
+            at = lanes_at(j, 256)
+            pre[...] = dot(act[...], wo[:, at])
+
+            def part(p):
+                rows = rows_at(p, PAIR)
+                store(p, at, stream[rows, at] + spread(valid[rows, :], 256) * (pre[rows, :] + vec[40 + k : 41 + k, at]))
+
+            each(pairs, part)
+
+        each(width // 256, tile2)
+
+    def into_pad(p, at, value):
+        pad[pl.ds(pl.multiple_of((18 * p + 1) * 8, 8), CELLS), at] = value[:CELLS]
+        pad[pl.ds(pl.multiple_of((18 * p + 10) * 8, 8), CELLS), at] = value[CELLS:]
+
+    convolve(0, streams.at[0])
+    save("pad0", pad, o_pad.at[0], 0)
+    save("s1", streams.at[0], o_stream.at[0], 1)
+    norm_rows(streams.at[0], images, vec, 0, normed.at[0])
+    save("n1", normed.at[0], o_normed.at[0], 2)
+    loads["q0"].wait()
+    qkv(0, normed.at[0])
+    save("k1", packed, o_packed.at[0], 3)
+    reload("q1", qkv1, wq, 0)
+    window_attention(packed, images, sizes, wr, wc, context)
+    save("c1", context, o_context.at[0], 4)
+    loads["p0"].wait()
+    saves["pad0"].wait()
+    proj(0, streams.at[0], into_pad)
+    reload("p1", proj1, wp, 1)
+    convolve(1, streams.at[1])
+    save("pad2", pad, o_pad.at[1], 0)
+    save("s3", streams.at[1], o_stream.at[1], 5)
+    norm_rows(streams.at[1], images, vec, 1, normed.at[1])
+    save("n3", normed.at[1], o_normed.at[1], 6)
+    loads["h0"].wait()
+    loads["o0"].wait()
+    saves["pad2"].wait()
+    feed_forward(0, normed.at[1], streams.at[1], into_pad)
+    save("a0", act, o_act.at[0], 7)
+    save("g0", slope, o_slope.at[0], 8)
+    reload("h1", hid1, wh, 2)
+    reload("o1", outw1, wo, 3)
+    saves["s1"].wait()
+    saves["n1"].wait()
+    saves["k1"].wait()
+    saves["c1"].wait()
+    convolve(2, streams.at[0])
+    save("pad4", pad, o_pad.at[2], 0)
+    save("s5", streams.at[0], o_stream.at[2], 1)
+    norm_rows(streams.at[0], images, vec, 2, normed.at[0])
+    save("n5", normed.at[0], o_normed.at[2], 2)
+    loads["q1"].wait()
+    qkv(1, normed.at[0])
+    save("k5", packed, o_packed.at[1], 3)
+    pair_grams(packed, 2 * width, packed, width, images, valid, gram)
+    sum_windows(gram, gram_in, images, wc, gram_sems, vertical, horizontal)
+
+    def soften(i):
+        rows = rows_at(i, 32)
+        x = gram[rows, :] * SCALE
+        e = jnp.exp(x - jnp.max(x, 0, keepdims=True))
+        gram[rows, :] = e * (1.0 / jnp.sum(e, 0, keepdims=True))
+
+    each(images, soften)
+    save("mix", gram, o_mix, 9)
+
+    def mix_pair(p):
+        rows = rows_at(p, PAIR)
+        one, two = image_halves(BF16)
+
+        def group(g):
+            at = lanes_at(g, 128)
+            a = unfold_heads(gram[pl.ds(pl.multiple_of(64 * p, 32), 32), at])
+            b = unfold_heads(gram[pl.ds(pl.multiple_of(64 * p + 32, 32), 32), at])
+            query = packed[rows, at]
+            mixing = jnp.concatenate([a, b], axis=0).astype(BF16)
+            context[rows, at] = dot(jnp.concatenate([query * one, query * two], axis=1), mixing).astype(BF16)
+
+        each(width // 128, group)
+
+    each(pairs, mix_pair)
+    save("c5", context, o_context.at[1], 4)
+    loads["p1"].wait()
+    saves["s3"].wait()
+    saves["n3"].wait()
+
+    def into_last(p, at, value):
+        streams[1, rows_at(p, PAIR), at] = value
+
+    proj(1, streams.at[0], into_last)
+    save("s6", streams.at[1], o_stream.at[3], 5)
+    norm_rows(streams.at[1], images, vec, 3, normed.at[1])
+    save("n6", normed.at[1], o_normed.at[3], 6)
+    loads["h1"].wait()
+    loads["o1"].wait()
+    saves["a0"].wait()
+    saves["g0"].wait()
+
+    def into_final(p, at, value):
+        final[rows_at(p, PAIR), at] = value.astype(BF16)
+
+    feed_forward(1, normed.at[1], streams.at[1], into_final)
+    save("a1", act, o_act.at[1], 7)
+    save("g1", slope, o_slope.at[1], 8)
+    save("end", final, activations, 10)
+    for name in ("pad4", "s5", "n5", "k5", "mix", "c5", "s6", "n6", "a1", "g1", "end"):
+        saves[name].wait()
+
+
+ANY = pl.BlockSpec(memory_space=pl.ANY)
+VMEM = pl.BlockSpec(memory_space=pltpu.VMEM)
+SMEM = pl.BlockSpec(memory_space=pltpu.SMEM)
+
+
+def run_forward(sizes, patches, vec, qbias, hbias, weights):
+    images = sizes.shape[0]
+    n_rows, width = patches.shape
+    hidden = hbias.shape[1]
+    lines = images * 72
+    shapes = (
+        ((n_rows, width), BF16),
+        ((3, lines, width), F32),
+        ((4, n_rows, width), F32),
+        ((4, n_rows, width), BF16),
+        ((2, n_rows, 3 * width), BF16),
+        ((2, n_rows, width), BF16),
+        ((2, n_rows, hidden), BF16),
+        ((2, n_rows, hidden), BF16),
+        ((images * 32, width), F32),
+    )
+    return pl.pallas_call(
+        functools.partial(forward_kernel, images, width, hidden),
+        out_shape=[jax.ShapeDtypeStruct(*s) for s in shapes],
+        in_specs=[SMEM, VMEM, VMEM, VMEM, VMEM] + [ANY] * 8,
+        out_specs=[ANY] * 9,
+        scratch_shapes=[
+            pltpu.VMEM((lines, width), F32),
+            pltpu.VMEM((2, n_rows, width), F32),
+            pltpu.VMEM((2, n_rows, width), BF16),
+            pltpu.VMEM((n_rows, 3 * width), BF16),
+            pltpu.VMEM((n_rows, width), BF16),
+            pltpu.VMEM((n_rows, hidden), BF16),
+            pltpu.VMEM((n_rows, hidden), BF16),
+            pltpu.VMEM((images * 32, width), F32),
+            pltpu.VMEM((3, images * 32, width), F32),
+            pltpu.VMEM((n_rows, 128), F32),
+            pltpu.VMEM((n_rows, 256), F32),
+            pltpu.VMEM((width, 3 * width), BF16),
+            pltpu.VMEM((width, width), BF16),
+            pltpu.VMEM((width, hidden), BF16),
+            pltpu.VMEM((hidden, width), BF16),
+            pltpu.VMEM((3, images * 8, width), BF16),
+            pltpu.VMEM((3, images * 8, width), BF16),
+            pltpu.VMEM((3, images * 8, width), BF16),
+            pltpu.VMEM((3, images * 8, width), BF16),
+            pltpu.VMEM((n_rows, width), BF16),
+            pltpu.SemaphoreType.DMA((3, 2, 2)),
+            pltpu.SemaphoreType.DMA((3, 2)),
+            pltpu.SemaphoreType.DMA((4,)),
+            pltpu.SemaphoreType.DMA((11,)),
+        ],
+        compiler_params=pltpu.CompilerParams(
+            collective_id=0, has_side_effects=True, vmem_limit_bytes=58 * 2**20
+        ),
+    )(sizes, patches, vec, qbias, hbias, *weights)
+
+
+def gathered(array, axis):
+    return lax.all_gather(array, "dp", axis=axis, tiled=True)
+
+
+def small_params(conv_weight, conv_bias, norm_gain, norm_bias, spatial_bias, channel_bias, proj_bias, hidden_bias, output_bias):
+    taps = conv_weight.reshape(-1, conv_weight.shape[-1])
+    rows = jnp.concatenate([taps, conv_bias, norm_gain, norm_bias, proj_bias, output_bias], axis=0)
+    vec = gathered(rows, 1)
+    spatial = gathered(spatial_bias, 0)
+    width = vec.shape[1]
+    zeros = jnp.zeros((width,), BF16)
+    qbias = jnp.stack(
+        [jnp.concatenate([spatial[:width], zeros, spatial[width:]]), gathered(channel_bias, 0)]
+    )
+    vec = jnp.pad(vec, ((0, -vec.shape[0] % 8), (0, 0)))
+    return vec.astype(F32), qbias.astype(F32), gathered(hidden_bias, 1).astype(F32)
+
+
+def to_cells(windows):
+    images, _, _, width = windows.shape
+    grid = windows.reshape(images, 7, 7, width)
+    return jnp.pad(grid, ((0, 0), (0, 0), (0, 1), (0, 0))).reshape(images * CELLS, width)
+
+
+def of_cells(rows, images):
+    width = rows.shape[1]
+    return rows.reshape(images, 7, 8, width)[:, :, :7].reshape(images, 1, 49, width)
+
+
+def on_device_fast(patches, cotangent, grid_sizes, conv_weight, conv_bias, norm_gain, norm_bias, qkv_weight, spatial_bias, channel_bias, proj_weight, proj_bias, hidden_weight, hidden_bias, output_weight, output_bias):
+    rest = on_device(patches, cotangent, grid_sizes, conv_weight, conv_bias, norm_gain, norm_bias, qkv_weight, spatial_bias, channel_bias, proj_weight, proj_bias, hidden_weight, hidden_bias, output_weight, output_bias)
+    vec, qbias, hbias = small_params(conv_weight, conv_bias, norm_gain, norm_bias, spatial_bias, channel_bias, proj_bias, hidden_bias, output_bias)
+    weights = [gathered(w, 1)[k] for w in (qkv_weight, proj_weight, hidden_weight, output_weight) for k in (0, 1)]
+    outs = run_forward(grid_sizes, to_cells(patches), vec, qbias, hbias, weights)
+    return (of_cells(outs[0], patches.shape[0]),) + tuple(rest[1:])
 
 
 def as_sent(array):
@@ -480,8 +1133,9 @@
 
 
 def solution(mesh):
+    small = mesh.shape["dp"] == 8 and mesh.shape["win"] == 4
     return jax.shard_map(
-        on_device,
+        on_device_fast if small else on_device,
         mesh=mesh,
         in_specs=(
             P("dp", "win", None, None),

time: 2650 us -> 2650 us (level)
  waiting for transfers between devices: 1540 us -> 1340 us
  Pallas kernels: 0 us -> 139 us
  local copies, waits for them, and re-layouts: 352 us -> 389 us
  blocking collectives: 283 us -> 314 us
    unnamed x29, waiting for transfers between devices: 190 us -> 2.74 us
    pallas_call x0 -> x1, Pallas kernels: none -> 139 us  [run_forward(): pl.pallas_call(functools.partial(forward_kernel, images, width, hidden),...]
    all_gather x1 -> x2, blocking collectives: 26.3 us -> 57.5 us  [gathered(): return lax.all_gather(array, 'dp', axis=axis, tiled=True)]
    dot_general x8 -> x7, matrix products: 76 us -> 66.5 us  [matmul(): return jnp.dot(left_rows, right_mat, preferred_element_type=jnp.float32)]
    unnamed x402 -> x457, local copies, waits for them, and re-layouts: 62 us -> 62.2 us
  transfers between devices with their start and end apart: 25 -> 25, of which waited for: 16 -> 12; matrix products, arithmetic and copies ran while one was open for 18% -> 19% of each run, Pallas kernels for 0% -> 5%
where the time goes in v1:
time: 2650 us; the launch traced here: 2640 us
  waiting for transfers between devices  1340 us (51%)
  local copies, waits for them, and re-layouts  389 us (15%)
  blocking collectives  314 us (12%)
  matrix products  219 us (8%)
  other arithmetic  206 us (8%)
  Pallas kernels  139 us (5%)
    reduce_scatter x1, waiting for transfers between devices, on_device(): lax.psum_scatter(jnp.stack([hid_w_grad0, hid_w_grad1]), 'dp', scatter_dim...  314 us
    reduce_scatter x1, waiting for transfers between devices, on_device(): lax.psum_scatter(jnp.stack([out_w_grad0, out_w_grad1]), 'dp', scatter_dim...  314 us
    reduce_scatter x1, waiting for transfers between devices, on_device(): lax.psum_scatter(jnp.stack([qkv_w_grad0, qkv_w_grad1]), 'dp', scatter_dim...  231 us
    all_gather x4, waiting for transfers between devices, gathered(): return lax.all_gather(array, 'dp', axis=axis, tiled=True)  211 us
    pallas_call x1, Pallas kernels, run_forward(): pl.pallas_call(functools.partial(forward_kernel, images, width, hidden),...  139 us
    reduce_scatter x1, waiting for transfers between devices, on_device(): lax.psum_scatter(jnp.stack([proj_w_grad0, proj_w_grad1]), 'dp', scatter_d...  83.1 us
    slice x2, local copies, waits for them, and re-layouts, position_conv(): weight9[tap_index]  77 us
    unnamed x2, blocking collectives  70.6 us
  transfers between devices with their start and end apart: 25, of which 12 were waited for; matrix products, arithmetic and copies ran while one was open for 19% of the time, Pallas kernels for 5%

profile of v1, /device:TPU:0, one launch (start us, length us, event | category | flops | bytes accessed | tf_op | source)
XLA Modules:
  0.0 2641.2 jit_solution(14252543865520376656)
XLA Ops:
  20.3 34.2 %all_gather.79 = bf16[3,9,768]{1,0,2:T(4,128)(2,1)S(1)} all-gather(bf16[3,9,96]{1,0,2:T(4,128)(2,1)S(1)} %copy.3706), channel_id=1, replica_groups=mesh['dp'=8,'win'=4] {'dp'}, dimensions={2}, use_global_device_ids=true | all-gather | bytes 46656 | tf_op jit(solution)/shard_map/all_gather | solution.py:886
  54.7 56.7 %slice_reduce_fusion.8 = (f32[768]{0:T(1024)}, f32[768]{0:T(1024)}, f32[768]{0:T(1024)}, f32[768]{0:T(1024)}, f32[768]{0:T(1024)}, /*index=5*/f32[768]{0:T(1024)...) fusion(f32[3,9,768]{1,0,2:T(4,128)S(1)} %convert_element_type.656), kind=kLoop, calls=%fused_computation.342 | loop fusion | bytes 116736 | tf_op jit(solution)/shard_map/slice | solution.py:749
  111.6 20.3 slice_reduce_fusion.26
  133.9 20.6 all-gather.1
  154.7 16.3 all-gather.3
  171.1 18.4 all-gather.2
  190.1 33.5 %all-reduce.7 = (bf16[1536]{0:T(1024)(128)(2,1)S(1)}, bf16[2304]{0:T(1024)(128)(2,1)}) all-reduce(bf16[1536]{0:T(1024)(128)(2,1)S(1)} %dynamic-update-slice, bf16[2304]{0:T(1024)(128)(2,1)S(1)} %dynamic-update-slice.1), channel_id=1, replica_groups=mesh['dp'=8,'win'=4] {'dp'}, use_global_device_ids=true, to_apply=%add.2 | all-reduce | flops 3840 | bytes 15360
  223.6 16.2 all-gather.4
  273.9 11.2 reshape.2579
  335.9 18.2 all-gather.5
  354.2 26.2 all_gather.74
  401.3 95.3 %all-gather.21.cloned.1.call-done = bf16[2,768,3072]{2,1,0:T(8,128)(2,1)} async-done(((bf16[2,96,3072]{2,1,0:T(8,128)(2,1)}), bf16[2,768,3072]{2,1,0:T(8,128)(2,1)}) %all-gather.21.cloned.1.call-update) | async-done | bytes 9437200 | tf_op jit(solution)/shard_map/all_gather | solution.py:630
  496.6 22.2 multiply_convert_fusion.2
  518.8 116.1 %all-gather.23.cloned.1.call-done = bf16[2,3072,768]{2,1,0:T(8,128)(2,1)} async-done(((bf16[2,384,768]{2,1,0:T(8,128)(2,1)}), bf16[2,3072,768]{2,1,0:T(8,128)(2,1)}) %all-gather.23.cloned.1.call-update) | async-done | bytes 9437200 | tf_op jit(solution)/shard_map/all_gather | solution.py:630
  647.5 20.0 all-gather.29.cloned.1.call-done
  709.0 46.8 %all-to-all-done = bf16[12,1,49,3,4,192]{5,2,3,1,0,4:T(8,128)(2,1)} async-done(((bf16[12,1,49,3,4,192]{5,2,3,1,0,4:T(8,128)(2,1)}), bf16[12,1,49,3,4,192]{5,2,3,1,0,4:T(8,128)(2,1)}, u32[]{:S(2)}, u32[]{:S(2)}) %all-to-all-start) | async-done | bytes 2709536 | tf_op jit(solution)/shard_map/all_to_all | solution.py:944
  755.8 10.5 copy.3784
  766.2 9.1 reshape.2501
  799.1 12.0 all-to-all-done.1
  819.6 20.1 fusion.5
  839.8 9.8 convert_reduce_fusion.2
  870.4 17.6 all-to-all-done.2
  917.0 9.5 pad_maximum_fusion.3
  926.5 11.9 copy.3793
  938.5 51.7 %all_to_all.60 = bf16[12,4,49,3,1,192]{5,2,4,3,0,1:T(8,128)(2,1)S(1)} all-to-all(bf16[12,4,49,3,1,192]{5,2,4,3,0,1:T(8,128)(2,1)} %copy.3793), channel_id=1, replica_groups=mesh['dp'=8,'win'=4] {'win'}, dimensions={1} | all-to-all | bytes 5419008 | tf_op jit(solution)/shard_map/all_to_all | solution.py:999
  1019.7 22.5 all-gather.31.cloned.1.call-done
  1059.7 11.0 convert_reduce_fusion.3
  1087.3 10.0 multiply_reduce_fusion.1
  1098.6 9.2 multiply_reduce_fusion.9
  1151.4 15.2 fusion.35
  1166.6 15.2 fusion.34
  1189.1 15.1 copy.3845
  1204.3 13.3 convert_element_type.721
  1229.0 9.3 multiply_reduce_fusion.17
  1257.7 8.6 convolution_bitcast_fusion.4
  1271.4 11.0 pad_maximum_fusion.2
  1301.8 8.2 convolution_bitcast_fusion
  1329.2 31.2 %all-gather = bf16[8,96,42]{1,2,0:T(8,128)(2,1)S(1)} all-gather(bf16[1,96,42]{1,2,0:T(8,128)(2,1)S(1)} %bitcast.813), channel_id=1, replica_groups=mesh['dp'=8,'win'=4] {'dp'}, dimensions={0}, use_global_device_ids=true | all-gather | bytes 72576 | tf_op jit(solution)/shard_map/all_gather | solution.py:630
  1372.8 8.2 slice_bitcast_fusion.2
  1381.0 8.1 slice_bitcast_fusion
  1389.1 139.3 %shard_map.271 = (bf16[672,768]{1,0:T(8,128)(2,1)}, f32[3,864,768]{2,1,0:T(8,128)}, f32[4,672,768]{2,1,0:T(8,128)}, bf16[4,672,768]{2,1,0:T(8,128)(2,1)}, bf16[2...) custom-call(s32[12]{0:T(128)} %sizes.1, ...), custom_call_target="tpu_custom_call" | custom-call | tf_op jit(solution)/shard_map/pallas_call | solution.py:592
  1535.8 37.2 %all-reduce.6 = (bf16[1536]{0:T(1024)(128)(2,1)S(1)}, bf16[2304]{0:T(1024)(128)(2,1)S(1)}) all-reduce(f32[1536]{0:T(1024)S(1)} %pad_maximum_fusion.36, f32[2304]{0:T(1024)S(1)} %reduce_sum.752), channel_id=7, replica_groups=mesh['dp'=8,'win'=4] {'dp'}, use_global_device_ids=true, to_apply=%region_71.72.clone | all-reduce | flops 3840 | bytes 23040
  1577.6 10.8 all-reduce.8
  1599.1 83.1 %reduce-scatter.28.cloned.1.call-done = f32[2,96,768]{2,1,0:T(8,128)} async-done(((f32[2,768,768]{2,1,0:T(8,128)}), f32[2,96,768]{2,1,0:T(8,128)}) %reduce-scatter.28.cloned.1.call-update) | async-done | bytes 589840 | tf_op jit(solution)/shard_map/reduce_scatter | solution.py:1098
  1684.0 231.3 %reduce-scatter.26.cloned.1.call-done = f32[2,96,2304]{2,1,0:T(8,128)} async-done(((f32[2,768,2304]{2,1,0:T(8,128)}), f32[2,96,2304]{2,1,0:T(8,128)}) %reduce-scatter.26.cloned.1.call-update) | async-done | bytes 1769488 | tf_op jit(solution)/shard_map/reduce_scatter | solution.py:1093
  1917.8 314.3 %reduce-scatter.30.cloned.1.call-done = f32[2,96,3072]{2,1,0:T(8,128)} async-done(((f32[2,768,3072]{2,1,0:T(8,128)}), f32[2,96,3072]{2,1,0:T(8,128)}) %reduce-scatter.30.cloned.1.call-update) | async-done | bytes 2359312 | tf_op jit(solution)/shard_map/reduce_scatter | solution.py:1104
  2234.9 314.1 %reduce-scatter.32.cloned.1.call-done = f32[2,384,768]{2,1,0:T(8,128)} async-done(((f32[2,3072,768]{2,1,0:T(8,128)}), f32[2,384,768]{2,1,0:T(8,128)}) %reduce-scatter.32.cloned.1.call-update) | async-done | bytes 2359312 | tf_op jit(solution)/shard_map/reduce_scatter | solution.py:1110
  2564.0 63.5 %all-reduce.12.cloned.1.call-done = (bf16[2,96,2304]{2,1,0:T(8,128)(2,1)}, bf16[2,96,768]{2,1,0:T(8,128)(2,1)}, bf16[2,96,3072]{2,1,0:T(8,128)(2,1)}, bf16[2,384,768]{2,1,0:T(8,128)(2,1)}) async-done(((bf16[2,96,2304]{2,1,0:T(8,128)(2,1)}, bf16[2,96,768]{2,1,0:T(8,128)(2,1)}, bf16[2,96,3072]{2,1,0:T(8,128)(2,1)}, bf16[2,384,768]{2,1,0:T(8,128)(2,1)}), (bf16[2,96,2304]{2,1,0:T(8,128)(2,1)}, ...) | async-done | bytes 3538960 | tf_op jit(solution)/shard_map/psum | solution.py:1122
  (876 shorter events, 506.0 us)
Async XLA Ops:
  7.2 234.0 %all-gather.25.cloned.1.call-start = ((), (), s32[]{:S(2)}) async-start(), calls=%async_computation.19 | async-start | bytes 2580480 | tf_op jit(solution)/shard_map/all_gather | solution.py:742
  13.8 235.0 %copy-start.10 = (f32[12,7,7,768]{3,2,1,0:T(8,128)}, f32[12,7,7,768]{3,2,1,0:T(8,128)S(1)}, u32[]{:S(2)}) copy-start(f32[12,7,7,768]{3,2,1,0:T(8,128)S(1)} %get-tuple-element.537) | copy-start | bytes 5419012
  15.7 253.6 %all-gather.17.cloned.1.call-start = ((), (), s32[]{:S(2)}) async-start(), calls=%async_computation.15 | async-start | bytes 7962624 | tf_op jit(solution)/shard_map/all_gather | solution.py:630
  16.5 309.8 %all-gather.19.cloned.1.call-start = ((), (), s32[]{:S(2)}) async-start(), calls=%async_computation.16 | async-start | bytes 2654208 | tf_op jit(solution)/shard_map/all_gather | solution.py:630
  17.2 363.3 %all-gather.27.cloned.1.call-start = ((), (), s32[]{:S(2)}) async-start(), calls=%async_computation.20 | async-start | bytes 2580480 | tf_op jit(solution)/shard_map/all_gather | solution.py:742
  111.4 137.4 %copy-start.123 = (f32[768]{0:T(1024)}, f32[768]{0:T(1024)S(1)}, u32[]{:S(2)}) copy-start(f32[768]{0:T(1024)S(1)} %get-tuple-element.467) | copy-start | bytes 9220
  111.4 277.2 %copy-start.141 = (f32[768]{0:T(1024)}, f32[768]{0:T(1024)S(1)}, u32[]{:S(2)}) copy-start(f32[768]{0:T(1024)S(1)} %get-tuple-element.458) | copy-start | bytes 9220
  111.4 277.2 %copy-start.143 = (f32[768]{0:T(1024)}, f32[768]{0:T(1024)S(1)}, u32[]{:S(2)}) copy-start(f32[768]{0:T(1024)S(1)} %get-tuple-element.459) | copy-start | bytes 9220
  111.4 277.2 %copy-start.145 = (f32[768]{0:T(1024)}, f32[768]{0:T(1024)S(1)}, u32[]{:S(2)}) copy-start(f32[768]{0:T(1024)S(1)} %get-tuple-element.460) | copy-start | bytes 9220
  111.4 277.2 %copy-start.147 = (f32[768]{0:T(1024)}, f32[768]{0:T(1024)S(1)}, u32[]{:S(2)}) copy-start(f32[768]{0:T(1024)S(1)} %get-tuple-element.461) | copy-start | bytes 9220
  111.4 277.2 %copy-start.149 = (f32[768]{0:T(1024)}, f32[768]{0:T(1024)S(1)}, u32[]{:S(2)}) copy-start(f32[768]{0:T(1024)S(1)} %get-tuple-element.462) | copy-start | bytes 9220
  111.5 277.2 %copy-start.151 = (f32[768]{0:T(1024)}, f32[768]{0:T(1024)S(1)}, u32[]{:S(2)}) copy-start(f32[768]{0:T(1024)S(1)} %get-tuple-element.463) | copy-start | bytes 9220
  111.5 277.2 %copy-start.153 = (f32[768]{0:T(1024)}, f32[768]{0:T(1024)S(1)}, u32[]{:S(2)}) copy-start(f32[768]{0:T(1024)S(1)} %get-tuple-element.464) | copy-start | bytes 9220
  111.5 277.2 %copy-start.155 = (f32[768]{0:T(1024)}, f32[768]{0:T(1024)S(1)}, u32[]{:S(2)}) copy-start(f32[768]{0:T(1024)S(1)} %get-tuple-element.465) | copy-start | bytes 9220
  111.5 277.2 %copy-start.157 = (f32[768]{0:T(1024)}, f32[768]{0:T(1024)S(1)}, u32[]{:S(2)}) copy-start(f32[768]{0:T(1024)S(1)} %get-tuple-element.466) | copy-start | bytes 9220
  131.9 116.9 %copy-start.125 = (f32[768]{0:T(1024)}, f32[768]{0:T(1024)S(1)}, u32[]{:S(2)}) copy-start(f32[768]{0:T(1024)S(1)} %get-tuple-element.468) | copy-start | bytes 9220
  131.9 116.9 %copy-start.127 = (f32[768]{0:T(1024)}, f32[768]{0:T(1024)S(1)}, u32[]{:S(2)}) copy-start(f32[768]{0:T(1024)S(1)} %get-tuple-element.469) | copy-start | bytes 9220
  131.9 116.9 %copy-start.129 = (f32[768]{0:T(1024)}, f32[768]{0:T(1024)S(1)}, u32[]{:S(2)}) copy-start(f32[768]{0:T(1024)S(1)} %get-tuple-element.470) | copy-start | bytes 9220
  132.0 180.1 %copy-start.188 = (pred[12,49]{1,0:T(8,128)(4,1)}, pred[12,49]{1,0:T(8,128)(4,1)S(1)}, u32[]{:S(2)}) copy-start(pred[12,49]{1,0:T(8,128)(4,1)S(1)} %broadcast_compare_fusion.2) | copy-start | bytes 1768
  241.1 255.5 %copy-start.86 = (f32[768]{0:T(1024)}, f32[768]{0:T(1024)S(1)}, u32[]{:S(2)}) copy-start(f32[768]{0:T(1024)S(1)} %get-tuple-element.673) | copy-start | bytes 9220
  241.1 255.5 %copy-start.94 = (f32[768]{0:T(1024)}, f32[768]{0:T(1024)S(1)}, u32[]{:S(2)}) copy-start(f32[768]{0:T(1024)S(1)} %get-tuple-element.482) | copy-start | bytes 9220
  334.7 161.9 %all-gather.21.cloned.1.call-start = ((), (), s32[]{:S(2)}) async-start(), calls=%async_computation.17 | async-start | bytes 10616832 | tf_op jit(solution)/shard_map/all_gather | solution.py:630
  335.3 299.6 %all-gather.23.cloned.1.call-start = ((), (), s32[]{:S(2)}) async-start(), calls=%async_computation.18 | async-start | bytes 10616832 | tf_op jit(solution)/shard_map/all_gather | solution.py:630
  335.8 331.7 %all-gather.29.cloned.1.call-start = ((), (), s32[]{:S(2)}) async-start(), calls=%async_computation.21 | async-start | bytes 2580480 | tf_op jit(solution)/shard_map/all_gather | solution.py:742
  380.5 459.3 %copy-start.101 = (f32[1,3072]{1,0:T(1,128)}, f32[1,3072]{1,0:T(1,128)S(1)}, u32[]{:S(2)}) copy-start(f32[1,3072]{1,0:T(1,128)S(1)} %get-tuple-element.636) | copy-start | bytes 36868
  400.9 234.0 %copy-start.12 = (f32[588,768]{1,0:T(8,128)}, f32[588,768]{1,0:T(8,128)S(1)}, u32[]{:S(2)}) copy-start(f32[588,768]{1,0:T(8,128)S(1)} %get-tuple-element.535) | copy-start | bytes 5419012
  400.9 117.9 %copy-start.81 = (f32[588]{0:T(1024)}, f32[588]{0:T(1024)S(1)}, u32[]{:S(2)}) copy-start(f32[588]{0:T(1024)S(1)} %broadcast_multiply_fusion.7) | copy-start | bytes 7060
  401.2 117.6 %copy-start.113 = (f32[588]{0:T(1024)}, f32[588]{0:T(1024)S(1)}, u32[]{:S(2)}) copy-start(f32[588]{0:T(1024)S(1)} %multiply_reduce_fusion.39) | copy-start | bytes 7060
  401.3 117.5 %copy-start.90 = (f32[588]{0:T(1024)}, f32[588]{0:T(1024)S(1)}, u32[]{:S(2)}) copy-start(f32[588]{0:T(1024)S(1)} %fusion.176) | copy-start | bytes 7060
  703.3 52.5 %all-to-all-start = ((bf16[12,1,49,3,4,192]{5,2,3,1,0,4:T(8,128)(2,1)}), bf16[12,1,49,3,4,192]{5,2,3,1,0,4:T(8,128)(2,1)}, u32[]{:S(2)}, u32[]{:S(2)}) async-start(bf16[12,1,49,3,4,192]{5,2,3,1,0,4:T(8,128)(2,1)} %copy.3783), calls=%async_computation | async-start | bytes 8257536 | tf_op jit(solution)/shard_map/all_to_all | solution.py:944
  789.5 21.6 all-to-all-start.1
  796.3 214.9 %copy-start.11 = (f32[588,768]{1,0:T(8,128)}, f32[588,768]{1,0:T(8,128)S(1)}, u32[]{:S(2)}) copy-start(f32[588,768]{1,0:T(8,128)S(1)} %reshape.2489) | copy-start | bytes 5419012
  866.5 21.5 all-to-all-start.2
  870.0 172.2 %all-gather.31.cloned.1.call-start = ((), (), s32[]{:S(2)}) async-start(), calls=%async_computation.22 | async-start | bytes 2580480 | tf_op jit(solution)/shard_map/all_gather | solution.py:757
  1019.7 90.3 %all-gather.33.cloned.1.call-start = ((), (), s32[]{:S(2)}) async-start(), calls=%async_computation.23 | async-start | bytes 2580480 | tf_op jit(solution)/shard_map/all_gather | solution.py:757
  1082.9 450.8 %reduce-scatter.46.cloned.1.call-start = ((), (), s32[]{:S(2)}) async-start(), calls=%async_computation.35 | async-start | bytes 442368
  1107.8 426.7 %reduce-scatter.44.cloned.1.call-start = ((), (), s32[]{:S(2)}) async-start(), calls=%async_computation.34 | async-start | bytes 1769472
  1109.8 463.2 %reduce-scatter.42.cloned.1.call-start = ((), (), s32[]{:S(2)}) async-start(), calls=%async_computation.33 | async-start | bytes 442368
  1240.6 333.3 %reduce-scatter.36.cloned.1.call-start = ((), (), s32[]{:S(2)}) async-start(), calls=%async_computation.30 | async-start | bytes 442368
  1241.7 333.1 %reduce-scatter.38.cloned.1.call-start = ((), (), s32[]{:S(2)}) async-start(), calls=%async_computation.31 | async-start | bytes 442368
  1242.8 333.0 %reduce-scatter.40.cloned.1.call-start = ((), (), s32[]{:S(2)}) async-start(), calls=%async_computation.32 | async-start | bytes 442368
  1243.9 332.7 %reduce-scatter.34.cloned.1.call-start = ((), (), s32[]{:S(2)}) async-start(), calls=%async_computation.29 | async-start | bytes 442368
  1248.1 345.6 %all-gather.35.cloned.1.call-start = ((), (), s32[]{:S(2)}) async-start(), calls=%async_computation.24 | async-start | bytes 2580480 | tf_op jit(solution)/shard_map/all_gather | solution.py:757
  1250.6 431.6 %reduce-scatter.28.cloned.1.call-start = ((), (), s32[]{:S(2)}) async-start(), calls=%async_computation.26 | async-start | bytes 5308416 | tf_op jit(solution)/shard_map/reduce_scatter | solution.py:1098
  1257.0 658.3 %reduce-scatter.26.cloned.1.call-start = ((), (), s32[]{:S(2)}) async-start(), calls=%async_computation.25 | async-start | bytes 15925248 | tf_op jit(solution)/shard_map/reduce_scatter | solution.py:1093
  1282.4 949.6 %reduce-scatter.30.cloned.1.call-start = ((), (), s32[]{:S(2)}) async-start(), calls=%async_computation.27 | async-start | bytes 21233664 | tf_op jit(solution)/shard_map/reduce_scatter | solution.py:1104
  1301.1 1247.9 %reduce-scatter.32.cloned.1.call-start = ((), (), s32[]{:S(2)}) async-start(), calls=%async_computation.28 | async-start | bytes 21233664 | tf_op jit(solution)/shard_map/reduce_scatter | solution.py:1110
  1322.9 1304.5 %all-reduce.12.cloned.1.call-start = ((), (), s32[]{:S(2)}) async-start(), calls=%async_computation.36 | async-start | bytes 7077888 | tf_op jit(solution)/shard_map/psum | solution.py:1122
  (182 other events, 2271.9 us)
Sparse Core Ops, SparseCore 0:
  15.8 25.0 all-gather.24
  43.2 108.7 all-gather.16
  154.2 50.8 all-gather.18
  334.8 21.5 all-gather.26
  358.4 138.1 all-gather.20
  498.6 136.2 all-gather.22
  646.9 20.5 all-gather.28
  1019.8 22.3 all-gather.30
  1083.0 22.3 all-gather.32
  1108.6 61.3 reduce-scatter.45
  1173.4 63.7 reduce-scatter.43
  1240.8 61.6 reduce-scatter.41
  1306.0 60.3 reduce-scatter.35
  1369.9 60.4 reduce-scatter.37
  1433.9 60.4 reduce-scatter.39
  1498.5 60.3 reduce-scatter.33
  1561.0 21.4 all-gather.34
  1586.5 95.7 reduce-scatter.27
  1686.3 228.9 reduce-scatter.25
  1919.5 312.4 reduce-scatter.29
  2236.4 312.5 reduce-scatter.31
  2552.9 74.5 all-reduce.11

commit v2 on v1

--- a/solution.py
+++ b/solution.py
@@ -249,7 +249,7 @@
     return e * (1.0 / jnp.sum(e, -1, keepdims=True))
 
 
-def window_attention(packed, images, sizes, wr, wc, context):
+def window_attention(packed, images, sizes, wr, wc, context, between):
     width = context.shape[1]
 
     def pair(p):
@@ -267,7 +267,9 @@
 
         each(width // 128, group)
 
-    each(images // 2, pair)
+    for p in range(images // 2):
+        pair(p)
+        between(1)
 
 
 def image_halves(kind):
@@ -311,28 +313,108 @@
 def sum_windows(gram, ins, images, c, sems, vertical, horizontal):
     half = images * 16
     mine = pl.ds(pl.multiple_of(half * c, 32), half)
-
-    def add(ref, rows):
-        gram[rows, :] = gram[rows, :] + ref[rows, :]
-
-    copy = remote(gram, ins.at[0], sems.at[0], horizontal)
+    other = pl.ds(pl.multiple_of(half * (1 - c), 32), half)
+
+    def add(k):
+        def one(i):
+            rows = pl.ds(pl.multiple_of(half * c + 32 * i, 32), 32)
+            gram[rows, :] = gram[rows, :] + ins[k, rows_at(i, 32), :]
+
+        each(images // 2, one)
+
+    copy = remote(gram.at[other], ins.at[0], sems.at[0], horizontal)
     copy.start()
     copy.wait()
-    each(images, lambda i: add(ins.at[0], rows_at(i, 32)))
-    copy = remote(gram.at[mine], ins.at[1, mine], sems.at[1], vertical)
+    add(0)
+    copy = remote(gram.at[mine], ins.at[1], sems.at[1], vertical)
     copy.start()
     copy.wait()
-    each(images // 2, lambda i: add(ins.at[1], pl.ds(pl.multiple_of(half * c + 32 * i, 32), 32)))
-    copy = remote(gram.at[mine], ins.at[2, mine], sems.at[2], horizontal)
+    add(1)
+    copy = remote(gram.at[mine], ins.at[2], sems.at[2], horizontal)
     copy.start()
     copy.wait()
-    other = half * (1 - c)
 
     def take(i):
-        rows = pl.ds(pl.multiple_of(other + 32 * i, 32), 32)
-        gram[rows, :] = ins[2, rows, :]
+        gram[pl.ds(pl.multiple_of(half * (1 - c) + 32 * i, 32), 32), :] = ins[2, rows_at(i, 32), :]
 
     each(images // 2, take)
+
+
+ROWS_WIDE = 42
+ROWS_SMALL = 64
+SHORT = 96
+
+
+def join(pieces):
+    tiles = [None] * (SHORT * len(pieces) // 128)
+    lane = iota(pieces[0].shape, 1)
+    for i, piece in enumerate(pieces):
+        t, shift = divmod(SHORT * i, 128)
+        moved = pltpu.roll(piece, shift, 1) if shift else piece
+        head = jnp.where(lane >= shift, moved, 0.0)
+        tiles[t] = head if tiles[t] is None else tiles[t] + head
+        if shift > 128 - SHORT:
+            tiles[t + 1] = jnp.where(lane < shift - (128 - SHORT), moved, 0.0)
+    return tiles
+
+
+def cut(tiles):
+    lane = iota(tiles[0].shape, 1)
+    pieces = []
+    for i in range(128 * len(tiles) // SHORT):
+        t, shift = divmod(SHORT * i, 128)
+        piece = pltpu.roll(tiles[t], 128 - shift, 1) if shift else tiles[t]
+        if shift > 128 - SHORT:
+            piece = jnp.where(lane < 128 - shift, piece, pltpu.roll(tiles[t + 1], 128 - shift, 1))
+        pieces.append(piece)
+    return pieces
+
+
+def small_rows():
+    return ((42, 2, 0), (44, 3, 1), (47, 4, 2), (51, 4, 3))
+
+
+def unpack_small(gathered_small, vec, qbias, hbias):
+    blocks = [gathered_small[d].astype(F32) for d in range(gathered_small.shape[0])]
+    for t, tile in enumerate(join(blocks)):
+        vec[:, 128 * t : 128 * t + 128] = tile
+    width = vec.shape[1]
+    qbias[...] = jnp.zeros(qbias.shape, F32)
+    for first, count, row in small_rows():
+        lines = [
+            jnp.broadcast_to(block[first + r : first + r + 1], (8, 128)) for block in blocks for r in range(count)
+        ]
+        for t, tile in enumerate(join(lines)):
+            line = tile[0:1]
+            if row == 0:
+                at = 128 * t if 128 * t < width else 128 * t + width
+                qbias[0:1, at : at + 128] = line
+            elif row == 1:
+                qbias[1:2, 128 * t : 128 * t + 128] = line
+            else:
+                hbias[row - 2 : row - 1, 128 * t : 128 * t + 128] = line
+
+
+def pack_small(vecg, qbg, hbg, out):
+    width = vecg.shape[1]
+    for d, piece in enumerate(cut([vecg[:, 128 * t : 128 * t + 128] for t in range(width // 128)])):
+        out[d, 0 : vecg.shape[0]] = piece
+    for first, count, row in small_rows():
+        if row == 0:
+            at = [128 * t if 128 * t < width else 128 * t + width for t in range(2 * width // 128)]
+            lines = [qbg[0:1, a : a + 128] for a in at]
+        elif row == 1:
+            lines = [qbg[1:2, 128 * t : 128 * t + 128] for t in range(3 * width // 128)]
+        else:
+            lines = [hbg[row - 2 : row - 1, 128 * t : 128 * t + 128] for t in range(4 * width // 128)]
+        for i, piece in enumerate(cut([jnp.broadcast_to(line, (8, 128)) for line in lines])):
+            d, r = divmod(i, count)
+            out[d, first + r : first + r + 1] = piece[0:1]
+
+
+LINE = 4
+AHEAD = 4
+LAG = 1
 
 
 def forward_kernel(
@@ -341,18 +423,14 @@
     hidden,
     sizes,
     patches,
+    small,
+    qkv_s,
+    proj_s,
+    hid_s,
+    out_s,
+    activations,
+    o_w,
     vec,
-    qbias,
-    hbias,
-    qkv0,
-    qkv1,
-    proj0,
-    proj1,
-    hid0,
-    hid1,
-    outw0,
-    outw1,
-    activations,
     o_pad,
     o_stream,
     o_normed,
@@ -385,23 +463,162 @@
     gram_sems,
     load_sems,
     save_sems,
+    z_sems,
+    y_sems,
+    xa_sems,
+    xb_sems,
+    c_sems,
+    own_sems,
+    small_in,
+    qbias,
+    hbias,
+    small_sems,
 ):
     d, w, wr, wc = place()
-    n_rows = images * CELLS
     pairs = images // 2
     horizontal = (d, 2 * wr + 1 - wc)
     vertical = (d, 2 * (1 - wr) + wc)
-    greet([horizontal, vertical])
+    z, y = d // 2, d % 2
+    depth = qkv_s.shape[1]
+    others = [lax.rem(z + k, LINE) for k in range(1, LINE)]
+    in_line = [(2 * other + y, w) for other in others]
+    across = (2 * z + 1 - y, w)
+    alike = [(lax.rem(d + k, 2 * LINE), w) for k in range(1, 2 * LINE)]
+    greet([horizontal, vertical] + alike)
+    for peer in alike:
+        remote(small, small_in.at[d], small_sems, peer).start()
     left, right = side_masks(wr, wc)
 
-    loads = {}
-    for name, src, dst, s in (("q0", qkv0, wq, 0), ("p0", proj0, wp, 1), ("h0", hid0, wh, 2), ("o0", outw0, wo, 3)):
-        loads[name] = pltpu.make_async_copy(src, dst, load_sems.at[s])
-        loads[name].start()
-
-    def reload(name, src, dst, s):
-        loads[name] = pltpu.make_async_copy(src, dst, load_sems.at[s])
-        loads[name].start()
+    columns = pl.ds(pl.multiple_of(wc * (width // 2), 128), width // 2)
+
+    def split(t):
+        return t % 4 != 3
+
+    def rows_of(t):
+        return pl.ds(pl.multiple_of(wr * (depth // 2), 16), depth // 2) if split(t) else pl.ds(0, depth)
+
+    def shard(t, rows):
+        layer, j = t // 12, t % 12
+        base = (0, 0, 0, 0, 4, 4, 4, 4, 8, 8, 8, 8)[j]
+        if j >= 8:
+            start = (j - base) * depth
+            return out_s.at[layer, pl.ds(pl.multiple_of(start + rows.start, 16), rows.size), columns]
+        source = qkv_s if j < 3 else proj_s if j < 4 else hid_s
+        shift = 0 if j == 3 else (j - base) * width
+        return source.at[layer, rows, pl.ds(pl.multiple_of(shift + wc * (width // 2), 128), width // 2)]
+
+    def piece(t, z_at, y_at):
+        return o_w.at[t, z_at, y_at, rows_of(t), columns]
+
+    def send(src, dst, sems, peer):
+        remote(src, dst, sems, peer).start()
+
+    def arrived(ref, sems):
+        pltpu.make_async_copy(ref, ref, sems.at[1]).wait()
+
+    def left_here(ref, sems):
+        pltpu.make_async_copy(ref, ref, sems.at[0]).wait()
+
+    def all_left(t):
+        left_here(o_w.at[t, pl.ds(0, LINE - 1), y, rows_of(t), columns], z_sems.at[t])
+        left_here(piece(t, pl.ds(0, LINE), y), y_sems.at[t])
+        if split(t):
+            left_here(o_w.at[t, pl.ds(0, LINE - 1), y, rows_of(t), columns], xa_sems.at[t])
+            left_here(piece(t, pl.ds(0, LINE), 1 - y), xb_sems.at[t])
+        left_here(o_w.at[t, pl.ds(0, LINE), pl.ds(0, 2), pl.ds(0, depth), columns], c_sems.at[t])
+
+    def own_copy(t):
+        return pltpu.make_async_copy(
+            shard(t, pl.ds(0, depth)), o_w.at[t, z, y, pl.ds(0, depth), columns], own_sems.at[t]
+        )
+
+    def open_chunk(t):
+        own_copy(t).start()
+        for peer in in_line:
+            send(shard(t, rows_of(t)), piece(t, z, y), z_sems.at[t], peer)
+        send(shard(t, rows_of(t)), piece(t, z, y), y_sems.at[t], across)
+
+    def stage_a(t):
+        arrived(o_w.at[t, pl.ds(0, LINE - 1), y, rows_of(t), columns], z_sems.at[t])
+        for other in others:
+            send(piece(t, other, y), piece(t, other, y), y_sems.at[t], across)
+        if split(t):
+            for other in others:
+                send(piece(t, other, y), piece(t, other, y), xa_sems.at[t], vertical)
+
+    def stage_b(t):
+        beside = piece(t, pl.ds(0, LINE), 1 - y)
+        arrived(beside, y_sems.at[t])
+        if split(t):
+            send(beside, beside, xb_sems.at[t], vertical)
+
+    def stage_c(t):
+        own_copy(t).wait()
+        if split(t):
+            rows = pl.ds(pl.multiple_of((1 - wr) * (depth // 2), 16), depth // 2)
+            arrived(o_w.at[t, pl.ds(0, LINE - 1), y, rows, columns], xa_sems.at[t])
+            arrived(o_w.at[t, pl.ds(0, LINE), 1 - y, rows, columns], xb_sems.at[t])
+        half = o_w.at[t, pl.ds(0, LINE), pl.ds(0, 2), pl.ds(0, depth), columns]
+        send(half, half, c_sems.at[t], horizontal)
+
+    chunks = 24
+    kinds = ("q", "q", "q", "p", "h", "h", "h", "h", "o", "o", "o", "o")
+    busy = {"q": True, "p": True, "h": True, "o": True}
+    landed, waiting = set(), []
+    clock = [0]
+
+    def load_of(t):
+        j = t % 12
+        if j < 3:
+            dst = wq.at[:, :, :, pl.ds(j * width, width)]
+        elif j < 4:
+            dst = wp
+        elif j < 8:
+            dst = wh.at[:, :, :, pl.ds((j - 4) * width, width)]
+        else:
+            dst = wo.at[:, :, j - 8]
+        return pltpu.make_async_copy(o_w.at[t], dst, load_sems.at[t])
+
+    def stage_d(t):
+        other = pl.ds(pl.multiple_of((1 - wc) * (width // 2), 128), width // 2)
+        arrived(o_w.at[t, pl.ds(0, LINE), pl.ds(0, 2), pl.ds(0, depth), other], c_sems.at[t])
+        if t < 12 or not busy[kinds[t % 12]]:
+            load_of(t).start()
+            landed.add(t)
+        else:
+            waiting.append(t)
+
+    def advance(count):
+        for _ in range(count):
+            t = clock[0]
+            if t >= chunks + 3 * LAG:
+                return
+            if t < chunks:
+                stage_a(t)
+                if t + AHEAD < chunks:
+                    open_chunk(t + AHEAD)
+            if 0 <= t - LAG < chunks:
+                stage_b(t - LAG)
+            if 0 <= t - 2 * LAG < chunks:
+                stage_c(t - 2 * LAG)
+            if 0 <= t - 3 * LAG < chunks:
+                stage_d(t - 3 * LAG)
+            clock[0] += 1
+
+    def need(t):
+        while clock[0] <= t + 3 * LAG and clock[0] < chunks + 3 * LAG:
+            advance(1)
+        load_of(t).wait()
+
+    def release(kind):
+        busy[kind] = False
+        for t in [t for t in waiting if kinds[t % 12] == kind]:
+            load_of(t).start()
+            landed.add(t)
+            waiting.remove(t)
+
+    for t in range(AHEAD):
+        open_chunk(t)
 
     saves = {}
 
@@ -409,6 +626,7 @@
         saves[name] = pltpu.make_async_copy(src, dst, save_sems.at[s])
         saves[name].start()
 
+    small_in[d] = small[...]
     fill_valid(valid, sizes, images, wr, wc)
     clear_borders(pad, images)
 
@@ -417,22 +635,34 @@
         to_pad(pad, p, patches[rows, :].astype(F32) * spread(valid[rows, :], width))
 
     each(pairs, enter)
+    arrived(small_in.at[pl.ds(0, 2 * LINE - 1)], small_sems)
+    unpack_small(small_in, vec, qbias, hbias)
 
     def convolve(k, stream):
         halo(pad, images, wr, wc, row_out.at[k], row_in.at[k], col_out.at[k], col_in.at[k], halo_sems.at[k], vertical, horizontal)
         conv_forward(pad, images, vec, k, valid, stream, left, right)
 
+    def columns_of(weights, at):
+        block = weights[:, :, :, at]
+        return block.reshape(width, block.shape[-1])
+
     def qkv(k, x):
+        for part in range(3):
+            need(12 * k + part)
+
+            def tile(j):
+                at = lanes_at(j, 256, part * width)
+                packed[:, at] = (dot(x[...], columns_of(wq, at)) + qbias[k : k + 1, at]).astype(BF16)
+
+            each(width // 256, tile)
+        release("q")
+
+    def proj(k, stream, store):
+        need(12 * k + 3)
+
         def tile(j):
             at = lanes_at(j, 256)
-            packed[:, at] = (dot(x[...], wq[:, at]) + qbias[k : k + 1, at]).astype(BF16)
-
-        each(3 * width // 256, tile)
-
-    def proj(k, stream, store):
-        def tile(j):
-            at = lanes_at(j, 256)
-            pre[...] = dot(context[...], wp[:, at])
+            pre[...] = dot(context[...], columns_of(wp, at))
 
             def part(p):
                 rows = rows_at(p, PAIR)
@@ -441,25 +671,34 @@
             each(pairs, part)
 
         each(width // 256, tile)
+        release("p")
 
     def feed_forward(k, x, stream, store):
-        def tile(j):
-            at = lanes_at(j, 256)
-            pre[...] = dot(x[...], wh[:, at])
-
-            def part(p):
-                rows = rows_at(p, PAIR)
-                a, s = gelu_pair(pre[rows, :] + hbias[k : k + 1, at])
-                act[rows, at] = a.astype(BF16)
-                slope[rows, at] = s.astype(BF16)
-
-            each(pairs, part)
-
-        each(hidden // 256, tile)
+        for block in range(4):
+            need(12 * k + 4 + block)
+
+            def tile(j):
+                at = lanes_at(j, 256, block * width)
+                pre[...] = dot(x[...], columns_of(wh, at))
+
+                def part(p):
+                    rows = rows_at(p, PAIR)
+                    a, s = gelu_pair(pre[rows, :] + hbias[k : k + 1, at])
+                    act[rows, at] = a.astype(BF16)
+                    slope[rows, at] = s.astype(BF16)
+
+                each(pairs, part)
+
+            each(width // 256, tile)
+            advance(1)
+        release("h")
+        for block in range(4):
+            need(12 * k + 8 + block)
 
         def tile2(j):
             at = lanes_at(j, 256)
-            pre[...] = dot(act[...], wo[:, at])
+            block = wo[:, :, :, :, at]
+            pre[...] = dot(act[...], block.reshape(hidden, 256))
 
             def part(p):
                 rows = rows_at(p, PAIR)
@@ -468,6 +707,7 @@
             each(pairs, part)
 
         each(width // 256, tile2)
+        release("o")
 
     def into_pad(p, at, value):
         pad[pl.ds(pl.multiple_of((18 * p + 1) * 8, 8), CELLS), at] = value[:CELLS]
@@ -478,29 +718,21 @@
     save("s1", streams.at[0], o_stream.at[0], 1)
     norm_rows(streams.at[0], images, vec, 0, normed.at[0])
     save("n1", normed.at[0], o_normed.at[0], 2)
-    loads["q0"].wait()
     qkv(0, normed.at[0])
     save("k1", packed, o_packed.at[0], 3)
-    reload("q1", qkv1, wq, 0)
-    window_attention(packed, images, sizes, wr, wc, context)
+    window_attention(packed, images, sizes, wr, wc, context, advance)
     save("c1", context, o_context.at[0], 4)
-    loads["p0"].wait()
     saves["pad0"].wait()
     proj(0, streams.at[0], into_pad)
-    reload("p1", proj1, wp, 1)
     convolve(1, streams.at[1])
     save("pad2", pad, o_pad.at[1], 0)
     save("s3", streams.at[1], o_stream.at[1], 5)
     norm_rows(streams.at[1], images, vec, 1, normed.at[1])
     save("n3", normed.at[1], o_normed.at[1], 6)
-    loads["h0"].wait()
-    loads["o0"].wait()
     saves["pad2"].wait()
     feed_forward(0, normed.at[1], streams.at[1], into_pad)
     save("a0", act, o_act.at[0], 7)
     save("g0", slope, o_slope.at[0], 8)
-    reload("h1", hid1, wh, 2)
-    reload("o1", outw1, wo, 3)
     saves["s1"].wait()
     saves["n1"].wait()
     saves["k1"].wait()
@@ -510,7 +742,6 @@
     save("s5", streams.at[0], o_stream.at[2], 1)
     norm_rows(streams.at[0], images, vec, 2, normed.at[0])
     save("n5", normed.at[0], o_normed.at[2], 2)
-    loads["q1"].wait()
     qkv(1, normed.at[0])
     save("k5", packed, o_packed.at[1], 3)
     pair_grams(packed, 2 * width, packed, width, images, valid, gram)
@@ -541,7 +772,6 @@
 
     each(pairs, mix_pair)
     save("c5", context, o_context.at[1], 4)
-    loads["p1"].wait()
     saves["s3"].wait()
     saves["n3"].wait()
 
@@ -552,8 +782,6 @@
     save("s6", streams.at[1], o_stream.at[3], 5)
     norm_rows(streams.at[1], images, vec, 3, normed.at[1])
     save("n6", normed.at[1], o_normed.at[3], 6)
-    loads["h1"].wait()
-    loads["o1"].wait()
     saves["a0"].wait()
     saves["g0"].wait()
 
@@ -564,6 +792,10 @@
     save("a1", act, o_act.at[1], 7)
     save("g1", slope, o_slope.at[1], 8)
     save("end", final, activations, 10)
+    advance(chunks + 3 * LAG)
+    for t in range(chunks):
+        all_left(t)
+    left_here(small_in.at[pl.ds(0, 2 * LINE - 1)], small_sems)
     for name in ("pad4", "s5", "n5", "k5", "mix", "c5", "s6", "n6", "a1", "g1", "end"):
         saves[name].wait()
 
@@ -573,13 +805,16 @@
 SMEM = pl.BlockSpec(memory_space=pltpu.SMEM)
 
 
-def run_forward(sizes, patches, vec, qbias, hbias, weights):
+def run_forward(sizes, patches, small, shards):
     images = sizes.shape[0]
     n_rows, width = patches.shape
-    hidden = hbias.shape[1]
+    hidden = shards[2].shape[2]
     lines = images * 72
+    depth = shards[0].shape[1]
     shapes = (
         ((n_rows, width), BF16),
+        ((24, LINE, 2, depth, width), BF16),
+        ((ROWS_SMALL, width), F32),
         ((3, lines, width), F32),
         ((4, n_rows, width), F32),
         ((4, n_rows, width), BF16),
@@ -592,8 +827,8 @@
     return pl.pallas_call(
         functools.partial(forward_kernel, images, width, hidden),
         out_shape=[jax.ShapeDtypeStruct(*s) for s in shapes],
-        in_specs=[SMEM, VMEM, VMEM, VMEM, VMEM] + [ANY] * 8,
-        out_specs=[ANY] * 9,
+        in_specs=[SMEM, VMEM, VMEM] + [ANY] * 4,
+        out_specs=[ANY] * 2 + [VMEM] + [ANY] * 8,
         scratch_shapes=[
             pltpu.VMEM((lines, width), F32),
             pltpu.VMEM((2, n_rows, width), F32),
@@ -603,13 +838,13 @@
             pltpu.VMEM((n_rows, hidden), BF16),
             pltpu.VMEM((n_rows, hidden), BF16),
             pltpu.VMEM((images * 32, width), F32),
-            pltpu.VMEM((3, images * 32, width), F32),
+            pltpu.VMEM((3, images * 16, width), F32),
             pltpu.VMEM((n_rows, 128), F32),
             pltpu.VMEM((n_rows, 256), F32),
-            pltpu.VMEM((width, 3 * width), BF16),
-            pltpu.VMEM((width, width), BF16),
-            pltpu.VMEM((width, hidden), BF16),
-            pltpu.VMEM((hidden, width), BF16),
+            pltpu.VMEM((LINE, 2, depth, 3 * width), BF16),
+            pltpu.VMEM((LINE, 2, depth, width), BF16),
+            pltpu.VMEM((LINE, 2, depth, hidden), BF16),
+            pltpu.VMEM((LINE, 2, 4, depth, width), BF16),
             pltpu.VMEM((3, images * 8, width), BF16),
             pltpu.VMEM((3, images * 8, width), BF16),
             pltpu.VMEM((3, images * 8, width), BF16),
@@ -617,31 +852,700 @@
             pltpu.VMEM((n_rows, width), BF16),
             pltpu.SemaphoreType.DMA((3, 2, 2)),
             pltpu.SemaphoreType.DMA((3, 2)),
-            pltpu.SemaphoreType.DMA((4,)),
+            pltpu.SemaphoreType.DMA((24,)),
             pltpu.SemaphoreType.DMA((11,)),
+            pltpu.SemaphoreType.DMA((24, 2)),
+            pltpu.SemaphoreType.DMA((24, 2)),
+            pltpu.SemaphoreType.DMA((24, 2)),
+            pltpu.SemaphoreType.DMA((24, 2)),
+            pltpu.SemaphoreType.DMA((24, 2)),
+            pltpu.SemaphoreType.DMA((24,)),
+            pltpu.VMEM((2 * LINE, ROWS_SMALL, 128), BF16),
+            pltpu.VMEM((8, 3 * width), F32),
+            pltpu.VMEM((8, hidden), F32),
+            pltpu.SemaphoreType.DMA((2,)),
         ],
         compiler_params=pltpu.CompilerParams(
             collective_id=0, has_side_effects=True, vmem_limit_bytes=58 * 2**20
         ),
-    )(sizes, patches, vec, qbias, hbias, *weights)
-
-
-def gathered(array, axis):
-    return lax.all_gather(array, "dp", axis=axis, tiled=True)
-
-
-def small_params(conv_weight, conv_bias, norm_gain, norm_bias, spatial_bias, channel_bias, proj_bias, hidden_bias, output_bias):
-    taps = conv_weight.reshape(-1, conv_weight.shape[-1])
-    rows = jnp.concatenate([taps, conv_bias, norm_gain, norm_bias, proj_bias, output_bias], axis=0)
-    vec = gathered(rows, 1)
-    spatial = gathered(spatial_bias, 0)
-    width = vec.shape[1]
-    zeros = jnp.zeros((width,), BF16)
-    qbias = jnp.stack(
-        [jnp.concatenate([spatial[:width], zeros, spatial[width:]]), gathered(channel_bias, 0)]
-    )
-    vec = jnp.pad(vec, ((0, -vec.shape[0] % 8), (0, 0)))
-    return vec.astype(F32), qbias.astype(F32), gathered(hidden_bias, 1).astype(F32)
+    )(sizes, patches, small, *shards)
+
+
+def column_sums(src, images, width, store):
+    for part in range(src.shape[1] // width):
+        at = pl.ds(part * width, width)
+
+        def one(p, total):
+            x = src[rows_at(p, PAIR), at].astype(F32)
+            return total + jnp.sum(x.reshape(PAIR // 8, 8, width), axis=0)
+
+        total = lax.fori_loop(0, images // 2, one, jnp.zeros((8, width), F32))
+        store(at, jnp.sum(total, axis=0, keepdims=True))
+
+
+def norm_back(stream, images, vec, k, grad_normed, grad, vecg):
+    gain = vec[30 + k : 31 + k, :]
+    width = stream.shape[1]
+
+    def one(p, carry):
+        rows = rows_at(p, PAIR)
+        x = stream[rows, :]
+        dn = grad_normed[rows, :]
+        centered = x - jnp.mean(x, -1, keepdims=True)
+        rstd = lax.rsqrt(jnp.mean(centered * centered, -1, keepdims=True) + EPS)
+        xhat = centered * rstd
+        scaled = dn * gain
+        inner = jnp.mean(scaled * xhat, -1, keepdims=True)
+        grad[rows, :] = grad[rows, :] + rstd * (scaled - jnp.mean(scaled, -1, keepdims=True) - xhat * inner)
+        gains = jnp.sum((dn * xhat).reshape(PAIR // 8, 8, width), axis=0)
+        shifts = jnp.sum(dn.reshape(PAIR // 8, 8, width), axis=0)
+        return carry[0] + gains, carry[1] + shifts
+
+    zero = jnp.zeros((8, width), F32)
+    gains, shifts = lax.fori_loop(0, images // 2, one, (zero, zero))
+    vecg[30 + k : 31 + k, :] = jnp.sum(gains, axis=0, keepdims=True)
+    vecg[34 + k : 35 + k, :] = jnp.sum(shifts, axis=0, keepdims=True)
+
+
+def conv_back(grad_pad, pad, images, vec, k, valid, grad, vecg, left, right):
+    keep = jnp.where(iota((8, 128), 0) < 7, 1.0, 0.0).astype(F32)
+    for part in range(pad.shape[1] // 128):
+        at = pl.ds(part * 128, 128)
+        taps = [vec[9 * k + t : 9 * k + t + 1, at] for t in range(9)]
+
+        def one(i, sums):
+            back = three(grad_pad, i, at, left, right)
+            ahead = three(pad, i, at, left, right)
+            sums = list(sums)
+            for r in range(7):
+                own = back[r + 1][1] * keep
+                total = own
+                for t in range(9):
+                    total = total + taps[t] * back[r + 2 - t // 3][2 - t % 3]
+                    sums[t] = sums[t] + own * ahead[r + t // 3][t % 3]
+                sums[9] = sums[9] + own
+                to = pl.ds(pl.multiple_of((7 * i + r) * 8, 8), 8)
+                grad[to, at] = valid[to, :] * total
+            return tuple(sums)
+
+        sums = lax.fori_loop(0, images, one, tuple(jnp.zeros((8, 128), F32) for _ in range(10)))
+        for t in range(9):
+            vecg[9 * k + t : 9 * k + t + 1, at] = jnp.sum(sums[t], axis=0, keepdims=True)
+        vecg[27 + k : 28 + k, at] = jnp.sum(sums[9], axis=0, keepdims=True)
+
+
+def window_back(packed, images, sizes, wr, wc, grad_context, between):
+    width = grad_context.shape[1]
+
+    def pair(p):
+        rows = rows_at(p, PAIR)
+        allowed = jnp.concatenate([pair_mask(sizes, p, wr, wc).astype(F32)] * 4, axis=0) > 0.5
+        low = head_masks(BF16)
+        full = head_masks(F32)
+
+        def group(g):
+            at_q, at_k, at_v = (lanes_at(g, 128, n * width) for n in range(3))
+            key = packed[rows, at_k]
+            query_bd = stacked(packed[rows, at_q], low)
+            grad_bd = stacked(grad_context[rows, lanes_at(g, 128)], low)
+            probs = pair_probs(query_bd, key, allowed)
+            grad_probs = dot_t(grad_bd, packed[rows, at_v])
+            packed[rows, at_v] = t_dot(probs.astype(BF16), grad_bd).astype(BF16)
+            inner = jnp.sum(probs * grad_probs, -1, keepdims=True)
+            grad_scores = jnp.where(allowed, probs * (grad_probs - inner), 0.0).astype(BF16)
+            packed[rows, at_q] = (folded(dot(grad_scores, key), full) * SCALE).astype(BF16)
+            packed[rows, at_k] = (t_dot(grad_scores, query_bd) * SCALE).astype(BF16)
+
+        each(width // 128, group)
+
+    for p in range(images // 2):
+        pair(p)
+        between(1)
+
+
+def channel_back(packed, images, mix, grad_gram, valid, grad_context):
+    width = grad_context.shape[1]
+
+    def pair(p):
+        rows = rows_at(p, PAIR)
+        one, two = image_halves(BF16)
+        ok = valid[rows, :] * SCALE
+        first = pl.ds(pl.multiple_of(64 * p, 32), 32)
+        second = pl.ds(pl.multiple_of(64 * p + 32, 32), 32)
+
+        def both(ref, at, axis):
+            return jnp.concatenate(
+                [unfold_heads(ref[first, at]), unfold_heads(ref[second, at])], axis=axis
+            ).astype(BF16)
+
+        def split(value):
+            return jnp.concatenate([value * one, value * two], axis=1)
+
+        def group(g):
+            at = lanes_at(g, 128)
+            at_k, at_v = lanes_at(g, 128, width), lanes_at(g, 128, 2 * width)
+            key, value = packed[rows, at_k], packed[rows, at_v]
+            packed[rows, at] = dot_t(split(grad_context[rows, at]), both(mix, at, 1)).astype(BF16)
+            packed[rows, at_k] = (dot(split(value), both(grad_gram, at, 0)) * ok).astype(BF16)
+            packed[rows, at_v] = (dot_t(split(key), both(grad_gram, at, 1)) * ok).astype(BF16)
+
+        each(width // 128, group)
+
+    each(images // 2, pair)
+
+
+ORDER = (20, 21, 22, 23, 16, 17, 18, 19, 15, 12, 13, 14, 8, 9, 10, 11, 4, 5, 6, 7, 3, 0, 1, 2)
+RING = 4
+AHEAD_SUMS = 1
+HELD = 12
+WAIT = 1
+
+
+def backward_kernel(
+    images,
+    width,
+    hidden,
+    sizes,
+    cotangent,
+    vec,
+    i_pad,
+    i_stream,
+    i_normed,
+    i_packed,
+    i_context,
+    i_act,
+    i_slope,
+    i_mix,
+    i_w,
+    patches_grad,
+    tiny,
+    g_qkv,
+    g_proj,
+    g_hid,
+    g_out,
+    grad,
+    grad_pad,
+    pad,
+    stream,
+    normed,
+    packed,
+    context,
+    act,
+    slope,
+    dn,
+    branch,
+    gram,
+    mix,
+    gram_in,
+    valid,
+    w_wide,
+    w_tall,
+    row_out,
+    row_in,
+    col_out,
+    col_in,
+    go_out,
+    go_in,
+    held,
+    x_in,
+    y_in,
+    z_in,
+    part,
+    part_in,
+    whole,
+    whole_in,
+    stage,
+    halo_sems,
+    gram_sems,
+    load_sems,
+    stage_sems,
+    weight_sems,
+    sums_sems,
+    credits,
+    vecg,
+    qbg,
+    hbg,
+    small_out,
+    small_in,
+    small_sum,
+    small_sems,
+):
+    d, w, wr, wc = place()
+    depth = i_w.shape[3]
+    pairs = images // 2
+    horizontal = (d, 2 * wr + 1 - wc)
+    vertical = (d, 2 * (1 - wr) + wc)
+    z, y = d // 2, d % 2
+    others = [lax.rem(z + k, LINE) for k in range(1, LINE)]
+    in_line = [(2 * other + y, w) for other in others]
+    across = (2 * z + 1 - y, w)
+    alike = [(lax.rem(d + k, 2 * LINE), w) for k in range(1, 2 * LINE)]
+    windows = [(d, lax.rem(w + k, 4)) for k in range(1, 4)]
+    greet(alike + windows)
+    vecg[...] = jnp.zeros(vecg.shape, F32)
+    left, right = side_masks(wr, wc)
+    loads = {}
+    half = width // 2
+    rows_mine = pl.ds(pl.multiple_of(wr * (depth // 2), 16), depth // 2)
+    rows_other = pl.ds(pl.multiple_of((1 - wr) * (depth // 2), 16), depth // 2)
+    cols_mine = pl.ds(pl.multiple_of(wc * half, 128), half)
+    cols_other = pl.ds(pl.multiple_of((1 - wc) * half, 128), half)
+    chunks = len(ORDER)
+    halves = [n for n in range(chunks) if n % 2 == 0]
+
+    def post(n, kind, src, dst, peer):
+        copy = remote(src, dst, sums_sems.at[n, kind], peer)
+        copy.start()
+
+    def settle(n, kind, ref):
+        pltpu.make_async_copy(ref, ref, sums_sems.at[n, kind, 1]).wait()
+        pltpu.make_async_copy(ref, ref, sums_sems.at[n, kind, 0]).wait()
+
+    def credit(n, kind, peer):
+        if n + RING < chunks:
+            pl.semaphore_signal(credits.at[kind], inc=1, device_id=peer, device_id_type=MESH)
+
+    def take_credit(n, kind):
+        if n >= RING:
+            pl.semaphore_wait(credits.at[kind], 1)
+
+    def open_sum(n):
+        take_credit(n, 0)
+        post(n, 0, go_out.at[n % RING], go_in.at[n % RING], horizontal)
+
+    def sum_cores(n):
+        s, h = n % RING, n % HELD
+        settle(n, 0, go_in.at[s])
+
+        def add(i):
+            held[h, i // 2, i % 2] = held[h, i // 2, i % 2] + go_in[s, i // 2, i % 2]
+
+        each(2 * LINE, add)
+        credit(n, 0, horizontal)
+        if n in halves:
+            if n >= RING:
+                pl.semaphore_wait(credits.at[1], 1)
+            post(n, 1, held.at[h, :, :, rows_other], x_in.at[s], vertical)
+        else:
+            take_credit(n, 2)
+            post(n, 2, held.at[h, :, 1 - y], y_in.at[s], across)
+
+    def sum_x(n):
+        if n not in halves:
+            return
+        s, h = n % RING, n % HELD
+        settle(n, 1, x_in.at[s])
+
+        def add(i):
+            held[h, i // 2, i % 2, rows_mine] = held[h, i // 2, i % 2, rows_mine] + x_in[s, i // 2, i % 2]
+
+        each(2 * LINE, add)
+        credit(n, 1, vertical)
+        take_credit(n, 2)
+        post(n, 2, held.at[h, :, 1 - y, rows_mine], y_in.at[s, :, 0 : depth // 2], across)
+
+    def share(n):
+        return (rows_mine, depth // 2) if n in halves else (pl.ds(0, depth), depth)
+
+    def sum_y(n):
+        s, h = n % RING, n % HELD
+        rows, count = share(n)
+        settle(n, 2, y_in.at[s, :, 0:count])
+
+        def add(i):
+            held[h, i, y, rows] = held[h, i, y, rows] + y_in[s, i, 0:count]
+
+        each(LINE, add)
+        credit(n, 2, across)
+        for k in range(LINE - 1):
+            take_credit(n, 3 + k)
+        for k, (other, peer) in enumerate(zip(others, in_line)):
+            post(n, 3, held.at[h, other, y, rows], z_in.at[s, LINE - 2 - k, 0:count], peer)
+
+    def sum_z(n):
+        s, h = n % RING, n % HELD
+        rows, count = share(n)
+        settle(n, 3, z_in.at[s, :, 0:count])
+        total = held[h, z, y, rows].astype(F32)
+        for k in range(LINE - 1):
+            total = total + z_in[s, k, 0:count].astype(F32)
+        part[s, rows] = total.astype(BF16)
+        for k, peer in enumerate(in_line):
+            credit(n, 3 + LINE - 2 - k, peer)
+        take_credit(n, 6)
+        post(n, 4, part.at[s, rows], part_in.at[s, rows], vertical)
+
+    def sum_windows_x(n):
+        s = n % RING
+        if n in halves:
+            settle(n, 4, part_in.at[s, rows_other])
+            whole[s, rows_mine] = part[s, rows_mine]
+            whole[s, rows_other] = part_in[s, rows_other]
+        else:
+            settle(n, 4, part_in.at[s])
+            whole[s] = part[s] + part_in[s]
+        credit(n, 6, vertical)
+        take_credit(n, 7)
+        post(n, 5, whole.at[s], whole_in.at[s], horizontal)
+
+    def result_of(n):
+        layer, j = ORDER[n] // 12, ORDER[n] % 12
+        if j < 3:
+            return g_qkv.at[layer, :, pl.ds(j * width, width)]
+        if j < 4:
+            return g_proj.at[layer]
+        if j < 8:
+            return g_hid.at[layer, :, pl.ds((j - 4) * width, width)]
+        return g_out.at[layer, pl.ds((j - 8) * depth, depth)]
+
+    def write_out(n):
+        return pltpu.make_async_copy(stage.at[n % RING], result_of(n), stage_sems.at[n % RING])
+
+    def finish(n):
+        s = n % RING
+        settle(n, 5, whole_in.at[s])
+        if n >= RING:
+            write_out(n - RING).wait()
+        stage[s, :, cols_mine] = whole[s].astype(F32)
+        stage[s, :, cols_other] = whole_in[s].astype(F32)
+        credit(n, 7, horizontal)
+        write_out(n).start()
+
+    stages = (sum_cores, sum_x, sum_y, sum_z, sum_windows_x, finish)
+    made, clock = [0], [0]
+
+    def turn():
+        for lag in reversed(range(len(stages))):
+            n = clock[0] - lag * WAIT
+            if 0 <= n < chunks:
+                stages[lag](n)
+        clock[0] += 1
+
+    def pump(count):
+        for _ in range(count):
+            if clock[0] < made[0] - AHEAD_SUMS or (made[0] == chunks and clock[0] < chunks + len(stages) * WAIT):
+                turn()
+
+    def room(count):
+        while made[0] + count > RING + clock[0] or made[0] + count - HELD > clock[0] - 3 * WAIT:
+            turn()
+
+    def opened(count):
+        for n in range(made[0], made[0] + count):
+            open_sum(n)
+        made[0] += count
+
+    def pair_of_halves(dy, base):
+        theirs = dy[:, pl.ds(pl.multiple_of(base + (1 - wc) * half, 128), half)]
+        ours = dy[:, pl.ds(pl.multiple_of(base + wc * half, 128), half)]
+        return jnp.concatenate([theirs, ours], axis=1)
+
+    def weight_grad(x, dy):
+        for j in range(dy.shape[1] // width):
+            room(1)
+            s, h = made[0] % RING, made[0] % HELD
+
+            def tile(q):
+                both = t_dot(x[:, lanes_at(q, 4 * depth)], pair_of_halves(dy, j * width)).astype(BF16)
+                go_out[s, rows_at(q, 2)] = both[:, :half].reshape(2, 2, depth, half)
+                held[h, rows_at(q, 2)] = both[:, half:].reshape(2, 2, depth, half)
+
+            each(LINE // 2, tile)
+            opened(1)
+            pump(1)
+
+    def tall_weight_grad(x, dy):
+        room(4)
+        slots = [(n % RING, n % HELD) for n in range(made[0], made[0] + 4)]
+
+        def tile(i):
+            both = t_dot(x[:, lanes_at(i, 4 * depth)], pair_of_halves(dy, 0)).astype(BF16)
+            for j, (s, h) in enumerate(slots):
+                block = both[j * depth : (j + 1) * depth]
+                go_out[s, i // 2, i % 2] = block[:, :half]
+                held[h, i // 2, i % 2] = block[:, half:]
+
+        each(2 * LINE, tile)
+        opened(4)
+        pump(1)
+
+    def load(name, src, dst, s):
+        loads[name] = pltpu.make_async_copy(src, dst, load_sems.at[s])
+        loads[name].start()
+
+    def load_weights(t):
+        j = t % 12
+        if j < 3:
+            dst = w_wide.at[:, :, :, pl.ds(j * width, width)]
+        elif j < 4:
+            dst = w_tall.at[:, :, 0]
+        elif j < 8:
+            dst = w_wide.at[:, :, :, pl.ds((j - 4) * width, width)]
+        else:
+            dst = w_tall.at[:, :, j - 8]
+        return pltpu.make_async_copy(i_w.at[t], dst, weight_sems.at[t])
+
+    def chunks_of(name):
+        first = {"wq": 0, "wp": 3, "wh": 4, "wo": 8}[name[:2]] + 12 * int(name[2])
+        return range(first, first + {"wq": 3, "wp": 1, "wh": 4, "wo": 4}[name[:2]])
+
+    def fetch(name):
+        for t in chunks_of(name):
+            load_weights(t).start()
+
+    def fetched(name):
+        for t in chunks_of(name):
+            load_weights(t).wait()
+
+    load("cotangent", cotangent, branch, 1)
+    load("act", i_act.at[1], act, 0)
+    fetch("wo1")
+    load("slope", i_slope.at[1], slope, 2)
+    fetch("wh1")
+    load("normed", i_normed.at[3], normed, 4)
+    load("stream", i_stream.at[3], stream, 5)
+    load("context", i_context.at[1], context, 6)
+    load("packed", i_packed.at[1], packed, 7)
+    load("mix", i_mix, mix, 8)
+    load("pad", i_pad.at[2], pad, 9)
+    fill_valid(valid, sizes, images, wr, wc)
+    clear_borders(grad_pad, images)
+
+    loads["cotangent"].wait()
+
+    def enter(p):
+        rows = rows_at(p, PAIR)
+        grad[rows, :] = branch[rows, :].astype(F32) * spread(valid[rows, :], width)
+
+    each(pairs, enter)
+
+    def make_branch(row):
+        def one(p):
+            rows = rows_at(p, PAIR)
+            branch[rows, :] = (grad[rows, :] * spread(valid[rows, :], width)).astype(BF16)
+
+        each(pairs, one)
+
+        def store(at, total):
+            vecg[row : row + 1, at] = total
+
+        column_sums(branch, images, 256, store)
+
+    def feed_forward(k):
+        make_branch(40 + k)
+        loads["act"].wait()
+        tall_weight_grad(act, branch)
+        fetched(f"wo{k}")
+        loads["slope"].wait()
+
+        def tile(j):
+            at = lanes_at(j, 4 * depth)
+            dact = dot_t(branch[...], w_tall[j // 2, j % 2].reshape(4 * depth, width))
+            slope[:, at] = (slope[:, at].astype(F32) * dact).astype(BF16)
+
+        each(2 * LINE, tile)
+        pump(1)
+
+        def store(at, total):
+            hbg[k : k + 1, at] = total
+
+        column_sums(slope, images, 256, store)
+        loads["normed"].wait()
+        weight_grad(normed, slope)
+        fetched(f"wh{k}")
+
+        def tile2(j):
+            block = w_wide[rows_at(j, 2)].reshape(4 * depth, hidden)
+            dn[:, lanes_at(j, 4 * depth)] = dot_t(slope[...], block)
+
+        each(LINE // 2, tile2)
+        pump(1)
+        loads["stream"].wait()
+        norm_back(stream, images, vec, 1 + 2 * k, dn, grad, vecg)
+
+    def proj(k):
+        make_branch(38 + k)
+        loads["context"].wait()
+        weight_grad(context, branch)
+        fetched(f"wp{k}")
+
+        def tile(j):
+            block = w_tall[rows_at(j, 2), :, 0].reshape(4 * depth, width)
+            context[:, lanes_at(j, 4 * depth)] = dot_t(branch[...], block).astype(BF16)
+
+        each(LINE // 2, tile)
+
+    def qkv(k):
+        def store(at, total):
+            qbg[k : k + 1, at] = total
+
+        column_sums(packed, images, 256, store)
+        loads["normed"].wait()
+        weight_grad(normed, packed)
+        fetched(f"wq{k}")
+
+        def tile(j):
+            block = w_wide[rows_at(j, 2), :, :, 0 : 3 * width].reshape(4 * depth, 3 * width)
+            dn[:, lanes_at(j, 4 * depth)] = dot_t(packed[...], block)
+
+        each(LINE // 2, tile)
+        loads["stream"].wait()
+        norm_back(stream, images, vec, 2 * k, dn, grad, vecg)
+
+    def convolve(k):
+        def enter_pad(p):
+            to_pad(grad_pad, p, grad[rows_at(p, PAIR), :])
+
+        each(pairs, enter_pad)
+        halo(grad_pad, images, wr, wc, row_out.at[k], row_in.at[k], col_out.at[k], col_in.at[k], halo_sems.at[k], vertical, horizontal)
+        loads["pad"].wait()
+        conv_back(grad_pad, pad, images, vec, k, valid, grad, vecg, left, right)
+
+    feed_forward(1)
+    load("act", i_act.at[0], act, 0)
+    load("slope", i_slope.at[0], slope, 2)
+    fetch("wp1")
+    fetch("wq1")
+    load("normed", i_normed.at[2], normed, 4)
+    load("stream", i_stream.at[2], stream, 5)
+    proj(1)
+    fetch("wo0")
+    loads["packed"].wait()
+    pair_grams(packed, 0, context, 0, images, valid, gram)
+    sum_windows(gram, gram_in, images, wc, gram_sems, vertical, horizontal)
+    loads["mix"].wait()
+
+    def harden(i):
+        rows = rows_at(i, 32)
+        y, g = mix[rows, :], gram[rows, :]
+        gram[rows, :] = y * (g - jnp.sum(y * g, 0, keepdims=True))
+
+    each(images, harden)
+    channel_back(packed, images, mix, gram, valid, context)
+    load("context", i_context.at[0], context, 6)
+    qkv(1)
+    fetch("wh0")
+    load("packed", i_packed.at[0], packed, 7)
+    load("normed", i_normed.at[1], normed, 4)
+    load("stream", i_stream.at[1], stream, 5)
+    convolve(2)
+    pump(1)
+    load("pad", i_pad.at[1], pad, 9)
+    feed_forward(0)
+    fetch("wp0")
+    fetch("wq0")
+    load("normed", i_normed.at[0], normed, 4)
+    load("stream", i_stream.at[0], stream, 5)
+    convolve(1)
+    pump(1)
+    load("pad", i_pad.at[0], pad, 9)
+    proj(0)
+    loads["packed"].wait()
+    window_back(packed, images, sizes, wr, wc, context, pump)
+    qkv(0)
+    convolve(0)
+
+    def leave(p):
+        rows = rows_at(p, PAIR)
+        branch[rows, :] = grad[rows, :].astype(BF16)
+
+    each(pairs, leave)
+    load("end", branch, patches_grad, 1)
+    pack_small(vecg, qbg, hbg, small_out)
+    small_in[d] = small_out[d]
+    for peer in alike:
+        remote(small_out.at[peer[0]], small_in.at[d], small_sems.at[0], peer).start()
+    while clock[0] < chunks + len(stages) * WAIT:
+        turn()
+    for n in (1, 0):
+        seven = small_in.at[pl.ds(0, 2 * LINE - 1)]
+        pltpu.make_async_copy(seven, seven, small_sems.at[0, n]).wait()
+    total = small_in[0]
+    for k in range(1, 2 * LINE):
+        total = total + small_in[k]
+    small_sum[w] = total
+    for peer in windows:
+        remote(small_sum.at[w], small_sum.at[w], small_sems.at[1], peer).start()
+    for n in (1, 0):
+        three_of = small_sum.at[pl.ds(0, 3)]
+        pltpu.make_async_copy(three_of, three_of, small_sems.at[1, n]).wait()
+    tiny[...] = ((small_sum[0] + small_sum[1]) + small_sum[2]) + small_sum[3]
+    for n in range(chunks - RING, chunks):
+        write_out(n).wait()
+    loads["end"].wait()
+
+
+def run_backward(sizes, cotangent, vec, saved, weights, hidden):
+    images = sizes.shape[0]
+    depth = weights.shape[3]
+    n_rows, width = cotangent.shape
+    lines = images * 72
+    shapes = (
+        ((n_rows, width), BF16),
+        ((ROWS_SMALL, 128), F32),
+        ((2, depth, 3 * width), F32),
+        ((2, depth, width), F32),
+        ((2, depth, hidden), F32),
+        ((2, 4 * depth, width), F32),
+    )
+    half = width // 2
+    return pl.pallas_call(
+        functools.partial(backward_kernel, images, width, hidden),
+        out_shape=[jax.ShapeDtypeStruct(*s) for s in shapes],
+        in_specs=[SMEM, ANY, VMEM] + [ANY] * 9,
+        out_specs=[ANY, VMEM] + [ANY] * 4,
+        scratch_shapes=[
+            pltpu.VMEM((n_rows, width), F32),
+            pltpu.VMEM((lines, width), F32),
+            pltpu.VMEM((lines, width), F32),
+            pltpu.VMEM((n_rows, width), F32),
+            pltpu.VMEM((n_rows, width), BF16),
+            pltpu.VMEM((n_rows, 3 * width), BF16),
+            pltpu.VMEM((n_rows, width), BF16),
+            pltpu.VMEM((n_rows, hidden), BF16),
+            pltpu.VMEM((n_rows, hidden), BF16),
+            pltpu.VMEM((n_rows, width), F32),
+            pltpu.VMEM((n_rows, width), BF16),
+            pltpu.VMEM((images * 32, width), F32),
+            pltpu.VMEM((images * 32, width), F32),
+            pltpu.VMEM((3, images * 16, width), F32),
+            pltpu.VMEM((n_rows, 128), F32),
+            pltpu.VMEM((LINE, 2, depth, hidden), BF16),
+            pltpu.VMEM((LINE, 2, 4, depth, width), BF16),
+            pltpu.VMEM((3, images * 8, width), BF16),
+            pltpu.VMEM((3, images * 8, width), BF16),
+            pltpu.VMEM((3, images * 8, width), BF16),
+            pltpu.VMEM((3, images * 8, width), BF16),
+            pltpu.VMEM((RING, LINE, 2, depth, half), BF16),
+            pltpu.VMEM((RING, LINE, 2, depth, half), BF16),
+            pltpu.VMEM((HELD, LINE, 2, depth, half), BF16),
+            pltpu.VMEM((RING, LINE, 2, depth // 2, half), BF16),
+            pltpu.VMEM((RING, LINE, depth, half), BF16),
+            pltpu.VMEM((RING, LINE - 1, depth, half), BF16),
+            pltpu.VMEM((RING, depth, half), BF16),
+            pltpu.VMEM((RING, depth, half), BF16),
+            pltpu.VMEM((RING, depth, half), BF16),
+            pltpu.VMEM((RING, depth, half), BF16),
+            pltpu.VMEM((RING, depth, width), F32),
+            pltpu.SemaphoreType.DMA((3, 2, 2)),
+            pltpu.SemaphoreType.DMA((3, 2)),
+            pltpu.SemaphoreType.DMA((10,)),
+            pltpu.SemaphoreType.DMA((RING,)),
+            pltpu.SemaphoreType.DMA((24,)),
+            pltpu.SemaphoreType.DMA((24, 6, 2)),
+            pltpu.SemaphoreType.REGULAR((8,)),
+            pltpu.VMEM((48, width), F32),
+            pltpu.VMEM((8, 3 * width), F32),
+            pltpu.VMEM((8, hidden), F32),
+            pltpu.VMEM((2 * LINE, ROWS_SMALL, 128), F32),
+            pltpu.VMEM((2 * LINE, ROWS_SMALL, 128), F32),
+            pltpu.VMEM((4, ROWS_SMALL, 128), F32),
+            pltpu.SemaphoreType.DMA((2, 2)),
+        ],
+        compiler_params=pltpu.CompilerParams(
+            collective_id=1, has_side_effects=True, vmem_limit_bytes=60 * 2**20
+        ),
+    )(sizes, cotangent, vec, *saved, weights)
 
 
 def to_cells(windows):
@@ -655,12 +1559,54 @@
     return rows.reshape(images, 7, 8, width)[:, :, :7].reshape(images, 1, 49, width)
 
 
-def on_device_fast(patches, cotangent, grid_sizes, conv_weight, conv_bias, norm_gain, norm_bias, qkv_weight, spatial_bias, channel_bias, proj_weight, proj_bias, hidden_weight, hidden_bias, output_weight, output_bias):
-    rest = on_device(patches, cotangent, grid_sizes, conv_weight, conv_bias, norm_gain, norm_bias, qkv_weight, spatial_bias, channel_bias, proj_weight, proj_bias, hidden_weight, hidden_bias, output_weight, output_bias)
-    vec, qbias, hbias = small_params(conv_weight, conv_bias, norm_gain, norm_bias, spatial_bias, channel_bias, proj_bias, hidden_bias, output_bias)
-    weights = [gathered(w, 1)[k] for w in (qkv_weight, proj_weight, hidden_weight, output_weight) for k in (0, 1)]
-    outs = run_forward(grid_sizes, to_cells(patches), vec, qbias, hbias, weights)
-    return (of_cells(outs[0], patches.shape[0]),) + tuple(rest[1:])
+def on_device_fast(
+    patches,
+    cotangent,
+    grid_sizes,
+    conv_weight,
+    conv_bias,
+    norm_gain,
+    norm_bias,
+    qkv_weight,
+    spatial_bias,
+    channel_bias,
+    proj_weight,
+    proj_bias,
+    hidden_weight,
+    hidden_bias,
+    output_weight,
+    output_bias,
+):
+    images = patches.shape[0]
+    hidden = hidden_weight.shape[2]
+    small = (
+        conv_weight, conv_bias, norm_gain, norm_bias, proj_bias, output_bias, spatial_bias, channel_bias, hidden_bias
+    )
+    rows = jnp.concatenate([a.reshape(-1, SHORT) for a in small], axis=0)
+    rows = jnp.pad(rows, ((0, ROWS_SMALL - rows.shape[0]), (0, 128 - SHORT)))
+    weights = (qkv_weight, proj_weight, hidden_weight, output_weight)
+    forward = run_forward(grid_sizes, to_cells(patches), rows, weights)
+    activations, gathered_weights, vec, *saved = forward
+    back = run_backward(grid_sizes, to_cells(cotangent), vec, saved, gathered_weights, hidden)
+    grads, tiny, g_qkv, g_proj, g_hid, g_out = back
+    tiny = tiny[:, :SHORT]
+    return (
+        of_cells(activations, images),
+        of_cells(grads, images),
+        tiny[:27].reshape(3, 9, SHORT),
+        tiny[27:30],
+        tiny[30:34],
+        tiny[34:38],
+        g_qkv,
+        tiny[42:44].reshape(-1),
+        tiny[44:47].reshape(-1),
+        g_proj,
+        tiny[38:40],
+        g_hid,
+        tiny[47:55].reshape(2, -1),
+        g_out,
+        tiny[40:42],
+    )
 
 
 def as_sent(array):

time: 2650 us -> 564 us (0.21)
  waiting for transfers between devices: 1340 us -> 0 us
  Pallas kernels: 139 us -> 524 us
  local copies, waits for them, and re-layouts: 389 us -> 29.6 us
  blocking collectives: 314 us -> 0 us
  matrix products: 219 us -> 0 us
  other arithmetic: 206 us -> 0 us
    reduce_scatter x4 -> x0, waiting for transfers between devices: 943 us -> none  [the longest x1 314 us: on_device(): lax.psum_scatter(jnp.stack([hid_w_grad0, hid_w_grad1]), 'dp', scatter_dim...]
    pallas_call x0 -> x1, Pallas kernels: none -> 306 us  [run_backward(): pl.pallas_call(functools.partial(backward_kernel, images, width, hidden),...]
    all_gather x10 -> x0, waiting for transfers between devices: 254 us -> none  [the longest x4 211 us: gathered(): return lax.all_gather(array, 'dp', axis=axis, tiled=True)]
    dot_general x35 -> x0, matrix products: 219 us -> none  [the longest x7 66.5 us: matmul(): return jnp.dot(left_rows, right_mat, preferred_element_type=jnp.float32)]
    all_gather x8 -> x0, blocking collectives: 181 us -> none  [the longest x2 57.5 us: gathered(): return lax.all_gather(array, 'dp', axis=axis, tiled=True)]
    reshape x43 -> x8, local copies, waits for them, and re-layouts: 106 us -> 4.33 us  [the longest x4 2.37 us: on_device_fast(): rows = jnp.concatenate([a.reshape(-1, SHORT) for a in small], axis=0)]
    slice x32 -> x5, local copies, waits for them, and re-layouts: 95.4 us -> 5.35 us  [the longest x1 1.36 us: on_device_fast(): tiny[34:38]]
    pallas_call x1, Pallas kernels: 139 us -> 218 us  [run_forward(): pl.pallas_call(functools.partial(forward_kernel, images, width, hidden),...]
  transfers between devices with their start and end apart: 25 -> 0, of which waited for: 12 -> 0; matrix products, arithmetic and copies ran while one was open for 19% -> 0% of each run, Pallas kernels for 5% -> 0%
where the time goes in v2:
time: 564 us; the launch traced here: 554 us
  Pallas kernels  524 us (93%)
  local copies, waits for them, and re-layouts  29.6 us (5%)
    pallas_call x1, Pallas kernels, run_backward(): pl.pallas_call(functools.partial(backward_kernel, images, width, hidden),...  306 us
    pallas_call x1, Pallas kernels, run_forward(): pl.pallas_call(functools.partial(forward_kernel, images, width, hidden),...  218 us

profile of v2, /device:TPU:0, one launch (start us, length us, event | category | flops | bytes accessed | tf_op | source)
XLA Modules:
  0.0 554.5 jit_solution(10293733911858009326)
XLA Ops:
  0.6 0.0 copy-start.3
  0.7 0.8 reshape.81
  1.5 0.8 reshape.82
  2.2 0.8 reshape.83
  3.0 0.7 copy.33
  3.7 3.0 concatenate.3
  6.7 0.6 pad.12.small
  7.3 1.4 reshape.78
  8.8 1.1 pad.11
  9.9 0.0 copy-done.3
  9.9 0.3 reshape.86
  10.2 1.1 pad.13
  11.3 217.6 %shard_map.271 = (bf16[672,768]{1,0:T(8,128)(2,1)}, bf16[24,4,2,96,768]{4,3,2,1,0:T(8,128)(2,1)}, f32[64,768]{1,0:T(8,128)}, f32[3,864,768]{2,1,0:T(8,128)}, f32...) custom-call(s32[12]{0:T(128)} %sizes.3, ...), custom_call_target="tpu_custom_call" | custom-call | tf_op jit(solution)/shard_map/pallas_call | solution.py:827
  228.9 2.2 reshape.85
  231.2 306.1 %shard_map.272 = (bf16[672,768]{1,0:T(8,128)(2,1)}, f32[64,128]{1,0:T(8,128)}, f32[2,96,2304]{2,1,0:T(8,128)}, f32[2,96,768]{2,1,0:T(8,128)}, f32[2,96,3072]{2,1,0:T(8,128)}, /*index=5*/f32[2,384,768]{2,1,0:T(8,128)}) custom-call(s32[12]{0:T(128)} %sizes.3, bf16[672,768]{1,0:T(8,128)(2,1)} %bitcast.7, f32[64,768]{1,0:T(8,128)} %get-tuple-element.33.vec, ...), custom_call_target="tpu_custom_call" | custom-call | tf_op jit(solution)/shard_map/pallas_call | solution.py:1492
  537.3 0.0 copy-start.2
  537.3 2.4 reshape.89
  539.7 0.0 copy-start.4
  539.7 1.3 fusion
  541.0 0.6 reshape.91
  541.6 0.7 slice.52
  542.3 0.7 reshape.93
  543.0 1.4 fusion.2
  544.4 1.3 fusion.1
  545.6 0.7 slice.45
  546.3 0.7 reshape.92
  547.0 0.6 copy.34
  547.6 0.0 copy-done.2
  547.6 0.0 copy-start.1
  547.6 1.2 copy.39
  548.8 0.0 copy-done.4
  548.8 0.8 copy.40
  549.6 0.5 copy-done.1
  550.1 0.0 copy-start
  550.1 1.4 copy.41
  551.5 1.1 copy-done
  552.6 1.4 copy.42
  (2 shorter events, 0.0 us)
Async XLA Ops:
  0.6 9.3 %copy-start.3 = (bf16[12,1,49,768]{3,2,1,0:T(8,128)(2,1)S(1)}, bf16[12,1,49,768]{3,2,1,0:T(8,128)(2,1)}, u32[]{:S(2)}) copy-start(bf16[12,1,49,768]{3,2,1,0:T(8,128)(2,1)} %param.17) | copy-start | bytes 2709508
  537.3 10.3 %copy-start.2 = (f32[2,96,2304]{2,1,0:T(8,128)S(1)}, f32[2,96,2304]{2,1,0:T(8,128)}, u32[]{:S(2)}) copy-start(f32[2,96,2304]{2,1,0:T(8,128)} %get-tuple-element.107) | copy-start | bytes 5308420
  539.7 9.1 %copy-start.4 = (f32[2,96,768]{2,1,0:T(8,128)S(1)}, f32[2,96,768]{2,1,0:T(8,128)}, u32[]{:S(2)}) copy-start(f32[2,96,768]{2,1,0:T(8,128)} %get-tuple-element.110) | copy-start | bytes 1769476
  547.6 2.5 copy-start.1
  550.1 2.5 copy-start

commit v3 on v2

--- a/solution.py
+++ b/solution.py
@@ -16,6 +16,7 @@
 SCALE = HEAD ** (-0.5)
 CELLS = 56
 PAIR = 112
+GROUPS = 3
 
 
 def dot(left, right):
@@ -48,6 +49,16 @@
         return carry
 
     lax.fori_loop(0, count, step, 0)
+
+
+def each_few(count, few, load, compute, store):
+    def step(n):
+        inputs = [load(n * few + u) for u in range(few)]
+        results = [compute(*values) for values in inputs]
+        for u in range(few):
+            store(n * few + u, results[u])
+
+    each(count // few, step)
 
 
 def gelu_pair(pre):
@@ -92,7 +103,7 @@
     return jnp.concatenate([valid_rows] * (width // 128), axis=1)
 
 
-def halo(pad, images, wr, wc, row_out, row_in, col_out, col_in, sems, vertical, horizontal):
+def halo(pad, images, wr, wc, row_out, row_in, col_out, col_in, sems, vertical, horizontal, flights):
     edge = 7 - 6 * wr
 
     def pack(p):
@@ -103,6 +114,7 @@
     each(images // 2, pack)
     copy = remote(row_out, row_in, sems.at[0], vertical)
     copy.start()
+    flights[0]()
     copy.wait()
     border = 8 - 8 * wr
 
@@ -133,6 +145,7 @@
     each(images // 2, pack_col)
     copy = remote(col_out, col_in, sems.at[1], horizontal)
     copy.start()
+    flights[1]()
     copy.wait()
 
     def unpack_col(p):
@@ -258,14 +271,17 @@
         low = head_masks(BF16)
         full = head_masks(F32)
 
-        def group(g):
-            query = packed[rows, lanes_at(g, 128)]
-            key = packed[rows, lanes_at(g, 128, width)]
-            value = packed[rows, lanes_at(g, 128, 2 * width)]
+        def load(g):
+            return tuple(packed[rows, lanes_at(g, 128, n * width)] for n in range(3))
+
+        def compute(query, key, value):
             probs = pair_probs(stacked(query, low), key, allowed).astype(BF16)
-            context[rows, lanes_at(g, 128)] = folded(dot(probs, value), full).astype(BF16)
-
-        each(width // 128, group)
+            return folded(dot(probs, value), full).astype(BF16)
+
+        def store(g, result):
+            context[rows, lanes_at(g, 128)] = result
+
+        each_few(width // 128, GROUPS, load, compute, store)
 
     for p in range(images // 2):
         pair(p)
@@ -298,19 +314,23 @@
         ok = valid[rows, :].astype(BF16)
         one, two = one * ok, two * ok
 
-        def group(g):
-            a = left[rows, lanes_at(g, 128, left_base)]
-            b = right[rows, lanes_at(g, 128, right_base)]
+        def load(g):
+            return left[rows, lanes_at(g, 128, left_base)], right[rows, lanes_at(g, 128, right_base)]
+
+        def compute(a, b):
             both = t_dot(a, jnp.concatenate([b * one, b * two], axis=1))
-            out[pl.ds(pl.multiple_of(64 * p, 32), 32), lanes_at(g, 128)] = fold_heads(both[:, :128])
-            out[pl.ds(pl.multiple_of(64 * p + 32, 32), 32), lanes_at(g, 128)] = fold_heads(both[:, 128:])
-
-        each(out.shape[1] // 128, group)
+            return fold_heads(both[:, :128]), fold_heads(both[:, 128:])
+
+        def store(g, result):
+            out[pl.ds(pl.multiple_of(64 * p, 32), 32), lanes_at(g, 128)] = result[0]
+            out[pl.ds(pl.multiple_of(64 * p + 32, 32), 32), lanes_at(g, 128)] = result[1]
+
+        each_few(out.shape[1] // 128, GROUPS, load, compute, store)
 
     each(images // 2, pair)
 
 
-def sum_windows(gram, ins, images, c, sems, vertical, horizontal):
+def sum_windows(gram, ins, images, c, sems, vertical, horizontal, flights):
     half = images * 16
     mine = pl.ds(pl.multiple_of(half * c, 32), half)
     other = pl.ds(pl.multiple_of(half * (1 - c), 32), half)
@@ -324,14 +344,17 @@
 
     copy = remote(gram.at[other], ins.at[0], sems.at[0], horizontal)
     copy.start()
+    flights[0]()
     copy.wait()
     add(0)
     copy = remote(gram.at[mine], ins.at[1], sems.at[1], vertical)
     copy.start()
+    flights[1]()
     copy.wait()
     add(1)
     copy = remote(gram.at[mine], ins.at[2], sems.at[2], horizontal)
     copy.start()
+    flights[2]()
     copy.wait()
 
     def take(i):
@@ -413,8 +436,10 @@
 
 
 LINE = 4
-AHEAD = 4
-LAG = 1
+AHEAD = 2
+FIRST = 1
+LAGS_FIRST = (0, 1, 2, 3)
+LAGS = (0, 2, 4, 5)
 
 
 def forward_kernel(
@@ -565,7 +590,7 @@
     kinds = ("q", "q", "q", "p", "h", "h", "h", "h", "o", "o", "o", "o")
     busy = {"q": True, "p": True, "h": True, "o": True}
     landed, waiting = set(), []
-    clock = [0]
+    clock, opened = [0], [0]
 
     def load_of(t):
         j = t % 12
@@ -588,25 +613,28 @@
         else:
             waiting.append(t)
 
+    order = []
+    for t in range(chunks):
+        lags = LAGS_FIRST if t < FIRST else LAGS
+        for stage, lag in zip((stage_a, stage_b, stage_c, stage_d), lags):
+            order.append((t + lag, -lag, t, stage))
+    order.sort(key=lambda entry: entry[:2])
+    last_step = {t: max(step for step, _, u, _ in order if u == t) for t in range(chunks)}
+    final_step = max(last_step.values())
+
     def advance(count):
         for _ in range(count):
-            t = clock[0]
-            if t >= chunks + 3 * LAG:
-                return
-            if t < chunks:
-                stage_a(t)
-                if t + AHEAD < chunks:
-                    open_chunk(t + AHEAD)
-            if 0 <= t - LAG < chunks:
-                stage_b(t - LAG)
-            if 0 <= t - 2 * LAG < chunks:
-                stage_c(t - 2 * LAG)
-            if 0 <= t - 3 * LAG < chunks:
-                stage_d(t - 3 * LAG)
+            for step, _, t, stage in order:
+                if step == clock[0]:
+                    stage(t)
+                    if stage is stage_a:
+                        for ahead in range(max(opened[0], AHEAD), min(t + 1 + AHEAD, chunks)):
+                            open_chunk(ahead)
+                            opened[0] = ahead + 1
             clock[0] += 1
 
     def need(t):
-        while clock[0] <= t + 3 * LAG and clock[0] < chunks + 3 * LAG:
+        while clock[0] <= last_step[t]:
             advance(1)
         load_of(t).wait()
 
@@ -635,12 +663,18 @@
         to_pad(pad, p, patches[rows, :].astype(F32) * spread(valid[rows, :], width))
 
     each(pairs, enter)
+    advance(1)
     arrived(small_in.at[pl.ds(0, 2 * LINE - 1)], small_sems)
     unpack_small(small_in, vec, qbias, hbias)
+    advance(1)
+
+    def step():
+        advance(1)
 
     def convolve(k, stream):
-        halo(pad, images, wr, wc, row_out.at[k], row_in.at[k], col_out.at[k], col_in.at[k], halo_sems.at[k], vertical, horizontal)
+        halo(pad, images, wr, wc, row_out.at[k], row_in.at[k], col_out.at[k], col_in.at[k], halo_sems.at[k], vertical, horizontal, (step, step))
         conv_forward(pad, images, vec, k, valid, stream, left, right)
+        advance(1)
 
     def columns_of(weights, at):
         block = weights[:, :, :, at]
@@ -655,6 +689,7 @@
                 packed[:, at] = (dot(x[...], columns_of(wq, at)) + qbias[k : k + 1, at]).astype(BF16)
 
             each(width // 256, tile)
+            advance(1)
         release("q")
 
     def proj(k, stream, store):
@@ -671,6 +706,7 @@
             each(pairs, part)
 
         each(width // 256, tile)
+        advance(1)
         release("p")
 
     def feed_forward(k, x, stream, store):
@@ -706,7 +742,9 @@
 
             each(pairs, part)
 
-        each(width // 256, tile2)
+        for j in range(width // 256):
+            tile2(j)
+            advance(1)
         release("o")
 
     def into_pad(p, at, value):
@@ -717,6 +755,7 @@
     save("pad0", pad, o_pad.at[0], 0)
     save("s1", streams.at[0], o_stream.at[0], 1)
     norm_rows(streams.at[0], images, vec, 0, normed.at[0])
+    advance(1)
     save("n1", normed.at[0], o_normed.at[0], 2)
     qkv(0, normed.at[0])
     save("k1", packed, o_packed.at[0], 3)
@@ -728,6 +767,7 @@
     save("pad2", pad, o_pad.at[1], 0)
     save("s3", streams.at[1], o_stream.at[1], 5)
     norm_rows(streams.at[1], images, vec, 1, normed.at[1])
+    advance(1)
     save("n3", normed.at[1], o_normed.at[1], 6)
     saves["pad2"].wait()
     feed_forward(0, normed.at[1], streams.at[1], into_pad)
@@ -741,11 +781,12 @@
     save("pad4", pad, o_pad.at[2], 0)
     save("s5", streams.at[0], o_stream.at[2], 1)
     norm_rows(streams.at[0], images, vec, 2, normed.at[0])
+    advance(1)
     save("n5", normed.at[0], o_normed.at[2], 2)
     qkv(1, normed.at[0])
     save("k5", packed, o_packed.at[1], 3)
     pair_grams(packed, 2 * width, packed, width, images, valid, gram)
-    sum_windows(gram, gram_in, images, wc, gram_sems, vertical, horizontal)
+    sum_windows(gram, gram_in, images, wc, gram_sems, vertical, horizontal, (step, step, step))
 
     def soften(i):
         rows = rows_at(i, 32)
@@ -760,15 +801,20 @@
         rows = rows_at(p, PAIR)
         one, two = image_halves(BF16)
 
-        def group(g):
+        def load(g):
             at = lanes_at(g, 128)
-            a = unfold_heads(gram[pl.ds(pl.multiple_of(64 * p, 32), 32), at])
-            b = unfold_heads(gram[pl.ds(pl.multiple_of(64 * p + 32, 32), 32), at])
-            query = packed[rows, at]
-            mixing = jnp.concatenate([a, b], axis=0).astype(BF16)
-            context[rows, at] = dot(jnp.concatenate([query * one, query * two], axis=1), mixing).astype(BF16)
-
-        each(width // 128, group)
+            first = gram[pl.ds(pl.multiple_of(64 * p, 32), 32), at]
+            second = gram[pl.ds(pl.multiple_of(64 * p + 32, 32), 32), at]
+            return first, second, packed[rows, at]
+
+        def compute(first, second, query):
+            mixing = jnp.concatenate([unfold_heads(first), unfold_heads(second)], axis=0).astype(BF16)
+            return dot(jnp.concatenate([query * one, query * two], axis=1), mixing).astype(BF16)
+
+        def store(g, result):
+            context[rows, lanes_at(g, 128)] = result
+
+        each_few(width // 128, GROUPS, load, compute, store)
 
     each(pairs, mix_pair)
     save("c5", context, o_context.at[1], 4)
@@ -781,6 +827,7 @@
     proj(1, streams.at[0], into_last)
     save("s6", streams.at[1], o_stream.at[3], 5)
     norm_rows(streams.at[1], images, vec, 3, normed.at[1])
+    advance(1)
     save("n6", normed.at[1], o_normed.at[3], 6)
     saves["a0"].wait()
     saves["g0"].wait()
@@ -792,7 +839,7 @@
     save("a1", act, o_act.at[1], 7)
     save("g1", slope, o_slope.at[1], 8)
     save("end", final, activations, 10)
-    advance(chunks + 3 * LAG)
+    advance(final_step + 1 - clock[0])
     for t in range(chunks):
         all_left(t)
     left_here(small_in.at[pl.ds(0, 2 * LINE - 1)], small_sems)
@@ -943,20 +990,26 @@
         low = head_masks(BF16)
         full = head_masks(F32)
 
-        def group(g):
-            at_q, at_k, at_v = (lanes_at(g, 128, n * width) for n in range(3))
-            key = packed[rows, at_k]
-            query_bd = stacked(packed[rows, at_q], low)
-            grad_bd = stacked(grad_context[rows, lanes_at(g, 128)], low)
+        def load(g):
+            return [packed[rows, lanes_at(g, 128, n * width)] for n in range(3)] + [grad_context[rows, lanes_at(g, 128)]]
+
+        def compute(query, key, value, grad):
+            query_bd = stacked(query, low)
+            grad_bd = stacked(grad, low)
             probs = pair_probs(query_bd, key, allowed)
-            grad_probs = dot_t(grad_bd, packed[rows, at_v])
-            packed[rows, at_v] = t_dot(probs.astype(BF16), grad_bd).astype(BF16)
+            grad_probs = dot_t(grad_bd, value)
+            grad_value = t_dot(probs.astype(BF16), grad_bd).astype(BF16)
             inner = jnp.sum(probs * grad_probs, -1, keepdims=True)
             grad_scores = jnp.where(allowed, probs * (grad_probs - inner), 0.0).astype(BF16)
-            packed[rows, at_q] = (folded(dot(grad_scores, key), full) * SCALE).astype(BF16)
-            packed[rows, at_k] = (t_dot(grad_scores, query_bd) * SCALE).astype(BF16)
-
-        each(width // 128, group)
+            grad_query = (folded(dot(grad_scores, key), full) * SCALE).astype(BF16)
+            grad_key = (t_dot(grad_scores, query_bd) * SCALE).astype(BF16)
+            return grad_query, grad_key, grad_value
+
+        def store(g, result):
+            for n in range(3):
+                packed[rows, lanes_at(g, 128, n * width)] = result[n]
+
+        each_few(width // 128, GROUPS, load, compute, store)
 
     for p in range(images // 2):
         pair(p)
@@ -981,15 +1034,22 @@
         def split(value):
             return jnp.concatenate([value * one, value * two], axis=1)
 
-        def group(g):
+        def load(g):
             at = lanes_at(g, 128)
-            at_k, at_v = lanes_at(g, 128, width), lanes_at(g, 128, 2 * width)
-            key, value = packed[rows, at_k], packed[rows, at_v]
-            packed[rows, at] = dot_t(split(grad_context[rows, at]), both(mix, at, 1)).astype(BF16)
-            packed[rows, at_k] = (dot(split(value), both(grad_gram, at, 0)) * ok).astype(BF16)
-            packed[rows, at_v] = (dot_t(split(key), both(grad_gram, at, 1)) * ok).astype(BF16)
-
-        each(width // 128, group)
+            values = [packed[rows, lanes_at(g, 128, n * width)] for n in range(1, 3)]
+            return values + [grad_context[rows, at], both(mix, at, 1), both(grad_gram, at, 0), both(grad_gram, at, 1)]
+
+        def compute(key, value, grad, mixing, grad_tall, grad_wide):
+            grad_query = dot_t(split(grad), mixing).astype(BF16)
+            grad_key = (dot(split(value), grad_tall) * ok).astype(BF16)
+            grad_value = (dot_t(split(key), grad_wide) * ok).astype(BF16)
+            return grad_query, grad_key, grad_value
+
+        def store(g, result):
+            for n in range(3):
+                packed[rows, lanes_at(g, 128, n * width)] = result[n]
+
+        each_few(width // 128, GROUPS, load, compute, store)
 
     each(images // 2, pair)
 
@@ -998,7 +1058,7 @@
 RING = 4
 AHEAD_SUMS = 1
 HELD = 12
-WAIT = 1
+WAIT = 2
 
 
 def backward_kernel(
@@ -1127,7 +1187,7 @@
                 pl.semaphore_wait(credits.at[1], 1)
             post(n, 1, held.at[h, :, :, rows_other], x_in.at[s], vertical)
         else:
-            take_credit(n, 2)
+            take_credit(n, 8)
             post(n, 2, held.at[h, :, 1 - y], y_in.at[s], across)
 
     def sum_x(n):
@@ -1156,7 +1216,7 @@
             held[h, i, y, rows] = held[h, i, y, rows] + y_in[s, i, 0:count]
 
         each(LINE, add)
-        credit(n, 2, across)
+        credit(n, 2 if n in halves else 8, across)
         for k in range(LINE - 1):
             take_credit(n, 3 + k)
         for k, (other, peer) in enumerate(zip(others, in_line)):
@@ -1350,8 +1410,6 @@
             hbg[k : k + 1, at] = total
 
         column_sums(slope, images, 256, store)
-        loads["normed"].wait()
-        weight_grad(normed, slope)
         fetched(f"wh{k}")
 
         def tile2(j):
@@ -1363,15 +1421,27 @@
         loads["stream"].wait()
         norm_back(stream, images, vec, 1 + 2 * k, dn, grad, vecg)
 
+    def hidden_grad():
+        loads["normed"].wait()
+        weight_grad(normed, slope)
+
+    def proj_grad():
+        loads["context"].wait()
+        weight_grad(context, branch)
+
+    def qkv_grad():
+        loads["normed"].wait()
+        weight_grad(normed, packed)
+
+    grad_context = act.at[:, pl.ds(0, width)]
+
     def proj(k):
         make_branch(38 + k)
-        loads["context"].wait()
-        weight_grad(context, branch)
         fetched(f"wp{k}")
 
         def tile(j):
             block = w_tall[rows_at(j, 2), :, 0].reshape(4 * depth, width)
-            context[:, lanes_at(j, 4 * depth)] = dot_t(branch[...], block).astype(BF16)
+            grad_context[:, lanes_at(j, 4 * depth)] = dot_t(branch[...], block).astype(BF16)
 
         each(LINE // 2, tile)
 
@@ -1380,8 +1450,6 @@
             qbg[k : k + 1, at] = total
 
         column_sums(packed, images, 256, store)
-        loads["normed"].wait()
-        weight_grad(normed, packed)
         fetched(f"wq{k}")
 
         def tile(j):
@@ -1392,27 +1460,35 @@
         loads["stream"].wait()
         norm_back(stream, images, vec, 2 * k, dn, grad, vecg)
 
-    def convolve(k):
+    def convolve(k, *flights):
         def enter_pad(p):
             to_pad(grad_pad, p, grad[rows_at(p, PAIR), :])
 
         each(pairs, enter_pad)
-        halo(grad_pad, images, wr, wc, row_out.at[k], row_in.at[k], col_out.at[k], col_in.at[k], halo_sems.at[k], vertical, horizontal)
+        halo(grad_pad, images, wr, wc, row_out.at[k], row_in.at[k], col_out.at[k], col_in.at[k], halo_sems.at[k], vertical, horizontal, flights)
         loads["pad"].wait()
         conv_back(grad_pad, pad, images, vec, k, valid, grad, vecg, left, right)
 
+    def idle():
+        pump(1)
+
     feed_forward(1)
-    load("act", i_act.at[0], act, 0)
-    load("slope", i_slope.at[0], slope, 2)
     fetch("wp1")
     fetch("wq1")
-    load("normed", i_normed.at[2], normed, 4)
     load("stream", i_stream.at[2], stream, 5)
     proj(1)
     fetch("wo0")
     loads["packed"].wait()
-    pair_grams(packed, 0, context, 0, images, valid, gram)
-    sum_windows(gram, gram_in, images, wc, gram_sems, vertical, horizontal)
+    pair_grams(packed, 0, grad_context, 0, images, valid, gram)
+
+    def beside():
+        hidden_grad()
+        proj_grad()
+
+    sum_windows(gram, gram_in, images, wc, gram_sems, vertical, horizontal, (idle, beside, idle))
+    load("slope", i_slope.at[0], slope, 2)
+    load("normed", i_normed.at[2], normed, 4)
+    load("context", i_context.at[0], context, 6)
     loads["mix"].wait()
 
     def harden(i):
@@ -1421,29 +1497,29 @@
         gram[rows, :] = y * (g - jnp.sum(y * g, 0, keepdims=True))
 
     each(images, harden)
-    channel_back(packed, images, mix, gram, valid, context)
-    load("context", i_context.at[0], context, 6)
+    channel_back(packed, images, mix, gram, valid, grad_context)
+    load("act", i_act.at[0], act, 0)
     qkv(1)
     fetch("wh0")
+    load("stream", i_stream.at[1], stream, 5)
+    convolve(2, qkv_grad, idle)
+    load("pad", i_pad.at[1], pad, 9)
     load("packed", i_packed.at[0], packed, 7)
     load("normed", i_normed.at[1], normed, 4)
-    load("stream", i_stream.at[1], stream, 5)
-    convolve(2)
-    pump(1)
-    load("pad", i_pad.at[1], pad, 9)
     feed_forward(0)
     fetch("wp0")
     fetch("wq0")
+    load("stream", i_stream.at[0], stream, 5)
+    convolve(1, hidden_grad, idle)
+    load("pad", i_pad.at[0], pad, 9)
     load("normed", i_normed.at[0], normed, 4)
-    load("stream", i_stream.at[0], stream, 5)
-    convolve(1)
-    pump(1)
-    load("pad", i_pad.at[0], pad, 9)
     proj(0)
+    proj_grad()
     loads["packed"].wait()
-    window_back(packed, images, sizes, wr, wc, context, pump)
+    window_back(packed, images, sizes, wr, wc, grad_context, pump)
+    qkv_grad()
     qkv(0)
-    convolve(0)
+    convolve(0, idle, idle)
 
     def leave(p):
         rows = rows_at(p, PAIR)
@@ -1533,7 +1609,7 @@
             pltpu.SemaphoreType.DMA((RING,)),
             pltpu.SemaphoreType.DMA((24,)),
             pltpu.SemaphoreType.DMA((24, 6, 2)),
-            pltpu.SemaphoreType.REGULAR((8,)),
+            pltpu.SemaphoreType.REGULAR((9,)),
             pltpu.VMEM((48, width), F32),
             pltpu.VMEM((8, 3 * width), F32),
             pltpu.VMEM((8, hidden), F32),

time: 564 us -> 468 us (0.83)
  Pallas kernels: 524 us -> 429 us
    pallas_call x1, Pallas kernels: 306 us -> 235 us  [run_backward(): pl.pallas_call(functools.partial(backward_kernel, images, width, hidden),...]
    pallas_call x1, Pallas kernels: 218 us -> 194 us  [run_forward(): pl.pallas_call(functools.partial(forward_kernel, images, width, hidden),...]
where the time goes in v3:
time: 468 us; the launch traced here: 460 us
  Pallas kernels  429 us (92%)
  local copies, waits for them, and re-layouts  29.6 us (6%)
    pallas_call x1, Pallas kernels, run_backward(): pl.pallas_call(functools.partial(backward_kernel, images, width, hidden),...  235 us
    pallas_call x1, Pallas kernels, run_forward(): pl.pallas_call(functools.partial(forward_kernel, images, width, hidden),...  194 us

profile of v3, /device:TPU:0, one launch (start us, length us, event | category | flops | bytes accessed | tf_op | source)
XLA Modules:
  0.0 459.5 jit_solution(8507151697289434345)
XLA Ops:
  0.6 0.0 copy-start.3
  0.7 0.8 reshape.81
  1.5 0.8 reshape.82
  2.2 0.8 reshape.83
  3.0 0.7 copy.33
  3.7 3.0 concatenate.3
  6.7 0.6 pad.12.small
  7.3 1.4 reshape.78
  8.8 1.1 pad.11
  9.9 0.0 copy-done.3
  9.9 0.3 reshape.86
  10.2 1.1 pad.13
  11.3 193.9 %shard_map.271 = (bf16[672,768]{1,0:T(8,128)(2,1)}, bf16[24,4,2,96,768]{4,3,2,1,0:T(8,128)(2,1)}, f32[64,768]{1,0:T(8,128)}, f32[3,864,768]{2,1,0:T(8,128)}, f32...) custom-call(s32[12]{0:T(128)} %sizes.3, ...), custom_call_target="tpu_custom_call" | custom-call | tf_op jit(solution)/shard_map/pallas_call | solution.py:874
  205.3 2.2 reshape.85
  207.5 234.8 %shard_map.272 = (bf16[672,768]{1,0:T(8,128)(2,1)}, f32[64,128]{1,0:T(8,128)}, f32[2,96,2304]{2,1,0:T(8,128)}, f32[2,96,768]{2,1,0:T(8,128)}, f32[2,96,3072]{2,1,0:T(8,128)}, /*index=5*/f32[2,384,768]{2,1,0:T(8,128)}) custom-call(s32[12]{0:T(128)} %sizes.3, bf16[672,768]{1,0:T(8,128)(2,1)} %bitcast.7, f32[64,768]{1,0:T(8,128)} %get-tuple-element.33.vec, ...), custom_call_target="tpu_custom_call" | custom-call | tf_op jit(solution)/shard_map/pallas_call | solution.py:1568
  442.4 0.0 copy-start.2
  442.4 2.4 reshape.89
  444.7 0.0 copy-start.4
  444.7 1.3 fusion
  446.0 0.6 reshape.91
  446.7 0.7 slice.52
  447.4 0.7 reshape.93
  448.0 1.4 fusion.2
  449.4 1.3 fusion.1
  450.7 0.7 slice.45
  451.4 0.7 reshape.92
  452.0 0.6 copy.34
  452.7 0.0 copy-done.2
  452.7 0.0 copy-start.1
  452.7 1.2 copy.39
  453.9 0.0 copy-done.4
  453.9 0.8 copy.40
  454.7 0.5 copy-done.1
  455.2 0.0 copy-start
  455.2 1.4 copy.41
  456.6 1.1 copy-done
  457.7 1.4 copy.42
  (2 shorter events, 0.0 us)
Async XLA Ops:
  0.6 9.3 %copy-start.3 = (bf16[12,1,49,768]{3,2,1,0:T(8,128)(2,1)S(1)}, bf16[12,1,49,768]{3,2,1,0:T(8,128)(2,1)}, u32[]{:S(2)}) copy-start(bf16[12,1,49,768]{3,2,1,0:T(8,128)(2,1)} %param.17) | copy-start | bytes 2709508
  442.4 10.3 %copy-start.2 = (f32[2,96,2304]{2,1,0:T(8,128)S(1)}, f32[2,96,2304]{2,1,0:T(8,128)}, u32[]{:S(2)}) copy-start(f32[2,96,2304]{2,1,0:T(8,128)} %get-tuple-element.107) | copy-start | bytes 5308420
  444.7 9.1 %copy-start.4 = (f32[2,96,768]{2,1,0:T(8,128)S(1)}, f32[2,96,768]{2,1,0:T(8,128)}, u32[]{:S(2)}) copy-start(f32[2,96,768]{2,1,0:T(8,128)} %get-tuple-element.110) | copy-start | bytes 1769476
  452.7 2.5 copy-start.1
  455.2 2.5 copy-start
